TPU v7x, 256 devices: a whole 4x4x8 slice. The times are simulated.
256 devices in a mesh: lev: 4 (over x), var: 64 (over y, z, core).
Axes of the slice: x: 4, y: 4, z: 8, core: 2. Of those that a mesh axis runs over, the one named last changes fastest.
Arguments:
- ensemble: float32 [4, 128, 2048, 128], P('lev', 'var'), may hold values from -6 to 6
- obs_sites: int32 [4, 8], replicated, may hold values from 0 to 262143, as said below
- owner: int32 [4], replicated, may hold values from 0 to 255, as said below
- tile_mask: int32 [4, 64], replicated, may hold values from 0 to 1, as said below
- obs_values: float32 [4, 8], replicated, may hold values from -6 to 6
- obs_error: float32 [4, 8], replicated, may hold values from 0.2 to 2
Outputs:
- analysis: float32 [4, 128, 2048, 128], P('lev', 'var')
Inputs may be any that keep to these rules, and one draw needn't show every extreme that they name: owner[b] // 64 is the level of block b's observations and owner[b] % 64 their tile. `obs_sites`: the 8 sites of a block are distinct, and each lies in the block's tile: site // 128 // 32 == owner[b] % 64. tile_mask[b, t] is 1 exactly where |t - owner[b] % 64| <= 3.
All inputs are finite; a program needn't handle non-finite values.
Results may differ from a plain program's by a relative error of at most 0.0001.
Values sent between devices are 32-bit elements; how exact they have to be, the bound alone decides.
A program may use at most 320 MiB of HBM per device.

v0:
```python
import jax
import jax.numpy as jnp
from jax import lax
from jax.sharding import PartitionSpec as P


def from_root(array, axis, root):
    mine = lax.axis_index(axis) == root
    return lax.psum(jnp.where(mine, array, jnp.zeros_like(array)), axis)


def taper_weight(delta_x, delta_y, radius):
    return jnp.square(
        jnp.maximum(0.0, 1.0 - (delta_x * delta_x + delta_y * delta_y) / (radius * radius))
    )


def vertical(level_gap):
    return jnp.exp2(-jnp.abs(level_gap).astype(jnp.float32))


def obs_increment(current, observed, variance, members):
    centre = jnp.mean(current)
    anomaly = current - centre
    spread = jnp.sum(anomaly * anomaly) / (members - 1) + 1e-06
    shifts = (
        spread / (spread + variance) * (observed - centre)
        + (jnp.sqrt(variance / (spread + variance)) - 1.0) * anomaly
    )
    return (anomaly, shifts, (members - 1) * spread)


def assimilate(
    priors,
    row_x,
    row_y,
    row_level,
    row_mask,
    first,
    site_x,
    site_y,
    site_level,
    values,
    errors,
    radius,
):
    members = priors.shape[1]
    count = values.shape[0]
    row_factor = row_mask * vertical(row_level - site_level)
    empty = jnp.zeros((count, members), jnp.float32)

    def assimilate_one_obs(obs_index, loop_state):
        priors, anomalies, shifts_all, scales = loop_state
        current = lax.dynamic_index_in_dim(priors, first + obs_index, 0, keepdims=False)
        anomaly, shifts, scaled = obs_increment(
            current, values[obs_index], errors[obs_index], members
        )
        row_weight = row_factor * taper_weight(
            row_x - site_x[obs_index], row_y - site_y[obs_index], radius
        )
        regress = jnp.dot(priors, anomaly, precision=lax.Precision.HIGHEST)
        priors = priors + (row_weight * regress / scaled)[:, None] * shifts[None, :]
        anomalies = lax.dynamic_update_index_in_dim(anomalies, anomaly, obs_index, 0)
        shifts_all = lax.dynamic_update_index_in_dim(shifts_all, shifts, obs_index, 0)
        scales = scales.at[obs_index].set(scaled)
        return (priors, anomalies, shifts_all, scales)

    return lax.fori_loop(
        0, count, assimilate_one_obs, (priors, empty, empty, jnp.zeros((count,), jnp.float32))
    )


def serial_update(
    field, anomalies, shifts_all, scales, cell_x, cell_y, cell_factor, site_x, site_y, radius
):

    def serial_one_obs(obs_index, field):
        weight = cell_factor * taper_weight(
            cell_x - site_x[obs_index], cell_y - site_y[obs_index], radius
        )
        regress = jnp.dot(anomalies[obs_index], field, precision=lax.Precision.HIGHEST)
        return (
            field + shifts_all[obs_index][:, None] * (weight * regress / scales[obs_index])[None, :]
        )

    return lax.fori_loop(0, anomalies.shape[0], serial_one_obs, field)


def shards(ensemble, obs_sites, owner, tile_mask, obs_values, obs_error):
    var_count = lax.axis_size("var")
    var_index = lax.axis_index("var")
    level_index = lax.axis_index("lev")
    m_dev = ensemble.shape[1]
    x_all = ensemble.shape[2]
    y_all = ensemble.shape[3]
    tile_width = x_all // var_count
    members = m_dev * var_count
    blocks = obs_sites.shape[0]
    radius = jnp.float32(3 * tile_width)
    by_cells = lax.all_to_all(ensemble, "var", split_axis=2, concat_axis=1, tiled=True)
    field = by_cells.reshape(members, tile_width * y_all)
    position = jnp.arange(tile_width * y_all, dtype=jnp.int32)
    cell_x = (var_index * tile_width + position // y_all).astype(jnp.float32)
    cell_y = (position % y_all).astype(jnp.float32)
    site_x_int = obs_sites // y_all
    site_x = site_x_int.astype(jnp.float32)
    site_y = (obs_sites % y_all).astype(jnp.float32)
    site_level = owner // var_count
    site_tile = site_x_int // tile_width
    masks = tile_mask.astype(jnp.float32)
    for block_no in range(blocks):
        local_index = jnp.clip(
            (site_x_int[block_no] - var_index * tile_width) * y_all + obs_sites[block_no] % y_all,
            0,
            tile_width * y_all - 1,
        )
        picked = jnp.take(field, local_index, axis=1).T
        priors = from_root(picked, ("lev", "var"), owner[block_no])
        row_mask = masks[block_no][site_tile[block_no]]
        results = assimilate(
            priors,
            site_x[block_no],
            site_y[block_no],
            site_level[block_no],
            row_mask,
            0,
            site_x[block_no],
            site_y[block_no],
            site_level[block_no],
            obs_values[block_no],
            obs_error[block_no],
            radius,
        )
        anomalies = results[1]
        shifts_all = results[2]
        scales = results[3]
        mask_here = masks[block_no, var_index]
        cell_factor = mask_here * vertical(level_index - site_level[block_no])
        field = serial_update(
            field,
            anomalies,
            shifts_all,
            scales,
            cell_x,
            cell_y,
            cell_factor,
            site_x[block_no],
            site_y[block_no],
            radius,
        )
    return lax.all_to_all(
        field.reshape(1, members, tile_width, y_all), "var", split_axis=1, concat_axis=2, tiled=True
    )


def solution(mesh):
    in_specs = (P("lev", "var", None, None), P(), P(), P(), P(), P())
    out_specs = P("lev", "var", None, None)
    return jax.shard_map(shards, mesh=mesh, in_specs=in_specs, out_specs=out_specs, check_vma=False)
```

profile of v0, /device:TPU:1, one launch (start us, length us, event | category | flops | bytes accessed | tf_op | source)
XLA Modules:
  0.0 892.1 jit_solution(6383845693298381198)
XLA Ops:
  0.0 5.4 copy.23
  5.5 13.3 %all-to-all-start = ((f32[1,2,2048,128]{3,1,0,2:T(2,128)}), f32[1,2,2048,128]{3,1,0,2:T(2,128)S(1)}, u32[]{:S(2)}, u32[]{:S(2)}) async-start(f32[1,2,2048,128]{3,1,0,2:T(2,128)} %copy.23), calls=%async_computation | async-start | bytes 4194304 | tf_op jit(solution)/shard_map/all_to_all | solution.py:100
  31.4 38.6 %all-to-all-done = f32[1,2,2048,128]{3,1,0,2:T(2,128)S(1)} async-done(((f32[1,2,2048,128]{3,1,0,2:T(2,128)}), f32[1,2,2048,128]{3,1,0,2:T(2,128)S(1)}, u32[]{:S(2)}, u32[]{:S(2)}) %all-to-all-start) | async-done | bytes 2097184 | tf_op jit(solution)/shard_map/all_to_all | solution.py:100
  73.7 2.1 gather_fusion.4
  75.9 75.5 %psum.28 = f32[8,128]{1,0:T(8,128)S(1)} all-reduce(f32[8,128]{1,0:T(8,128)S(1)} %fusion.143), channel_id=1, replica_groups=mesh['lev'=4,'var'=64] {'lev','var'}, use_global_device_ids=true, to_apply=%region_0.2 | all-reduce | flops 1024 | bytes 8192 | tf_op jit(solution)/shard_map/psum | solution.py:9
  151.5 68.8 %while.144 = (s32[]{:T(128)}, f32[8,128]{1,0:T(8,128)S(1)}, f32[8,128]{1,0:T(8,128)S(1)}, f32[8,128]{1,0:T(8,128)S(1)}, f32[8]{0:T(128)S(1)}, /*index=5*/f32[8]{...) while((s32[]{:T(128)}, f32[8,128]{1,0:T(8,128)S(1)}, ...), condition=%wide.region_4.6_spmd, body=%wide.region_1.5_spmd.sunk | while | flops 15470 | bytes 19595 | solution.py:68
  220.3 42.6 %while.148 = (s32[]{:T(128)}, f32[128,4096]{1,0:T(8,128)S(1)}, f32[8,128]{1,0:T(8,128)S(1)}, f32[]{:T(128)}, f32[8]{0:T(128)S(1)}, /*index=5*/f32[8]{0:T(128)S(1...) while((s32[]{:T(128)}, f32[128,4096]{1,0:T(8,128)S(1)}, f32[8,128]{1,0:T(8,128)S(1)}, ...), condition=%wide.region_6.8_spmd.clone, body=%wide.region_5.7_spmd.clone.sunk | while | flops 7450626 | bytes 6359205 | solution.py:86
  223.2 1.9 fusion.241
  228.5 1.9 fusion.241
  233.8 1.9 fusion.241
  239.2 1.9 fusion.241
  264.7 2.1 gather_fusion.5
  266.9 73.3 %psum.29 = f32[8,128]{1,0:T(8,128)S(1)} all-reduce(f32[8,128]{1,0:T(8,128)S(1)} %fusion.142), channel_id=1, replica_groups=mesh['lev'=4,'var'=64] {'lev','var'}, use_global_device_ids=true, to_apply=%region_7.9 | all-reduce | flops 1024 | bytes 8192 | tf_op jit(solution)/shard_map/psum | solution.py:9
  340.2 69.8 %while.145 = (s32[]{:T(128)}, f32[8,128]{1,0:T(8,128)S(1)}, f32[8,128]{1,0:T(8,128)S(1)}, f32[8,128]{1,0:T(8,128)S(1)}, f32[8]{0:T(128)S(1)}, /*index=5*/f32[8]{...) while((s32[]{:T(128)}, f32[8,128]{1,0:T(8,128)S(1)}, ...), condition=%wide.region_11.13_spmd, body=%wide.region_8.12_spmd.sunk | while | flops 15470 | bytes 19595 | solution.py:68
  410.0 41.9 %while.149 = (s32[]{:T(128)}, f32[128,4096]{1,0:T(8,128)S(1)}, f32[8,128]{1,0:T(8,128)S(1)}, f32[]{:T(128)}, f32[8]{0:T(128)S(1)}, /*index=5*/f32[8]{0:T(128)S(1...) while((s32[]{:T(128)}, f32[128,4096]{1,0:T(8,128)S(1)}, ...), condition=%wide.region_13.15_spmd.clone, body=%wide.region_12.14_spmd.clone.sunk | while | flops 7450626 | bytes 6359205 | solution.py:86
  453.8 2.1 gather_fusion.6
  456.0 73.2 %psum.30 = f32[8,128]{1,0:T(8,128)S(1)} all-reduce(f32[8,128]{1,0:T(8,128)S(1)} %fusion.141), channel_id=1, replica_groups=mesh['lev'=4,'var'=64] {'lev','var'}, use_global_device_ids=true, to_apply=%region_14.16 | all-reduce | flops 1024 | bytes 8192 | tf_op jit(solution)/shard_map/psum | solution.py:9
  529.2 70.5 %while.146 = (s32[]{:T(128)}, f32[8,128]{1,0:T(8,128)S(1)}, f32[8,128]{1,0:T(8,128)S(1)}, f32[8,128]{1,0:T(8,128)S(1)}, f32[8]{0:T(128)S(1)}, /*index=5*/f32[8]{...) while((s32[]{:T(128)}, f32[8,128]{1,0:T(8,128)S(1)}, ...), condition=%wide.region_18.20_spmd, body=%wide.region_15.19_spmd.sunk | while | flops 15470 | bytes 19595 | solution.py:68
  599.7 43.3 %while.150 = (s32[]{:T(128)}, f32[128,4096]{1,0:T(8,128)S(1)}, f32[8,128]{1,0:T(8,128)S(1)}, f32[]{:T(128)}, f32[8]{0:T(128)S(1)}, /*index=5*/f32[8]{0:T(128)S(1...) while((s32[]{:T(128)}, f32[128,4096]{1,0:T(8,128)S(1)}, ...), condition=%wide.region_20.22_spmd.clone, body=%wide.region_19.21_spmd.clone.sunk | while | flops 7450626 | bytes 6359205 | solution.py:86
  602.7 2.0 fusion.249
  608.1 2.0 fusion.249
  613.5 2.0 fusion.249
  618.9 2.0 fusion.249
  624.3 2.0 fusion.249
  629.7 2.0 fusion.249
  635.1 2.0 fusion.249
  640.5 2.0 fusion.249
  644.8 2.1 gather_fusion.7
  647.0 74.1 %psum.31 = f32[8,128]{1,0:T(8,128)S(1)} all-reduce(f32[8,128]{1,0:T(8,128)S(1)} %fusion.140), channel_id=1, replica_groups=mesh['lev'=4,'var'=64] {'lev','var'}, use_global_device_ids=true, to_apply=%region_21.23 | all-reduce | flops 1024 | bytes 8192 | tf_op jit(solution)/shard_map/psum | solution.py:9
  721.1 69.0 %while.147 = (s32[]{:T(128)}, f32[8,128]{1,0:T(8,128)S(1)}, f32[8,128]{1,0:T(8,128)S(1)}, f32[8,128]{1,0:T(8,128)S(1)}, f32[8]{0:T(128)S(1)}, /*index=5*/f32[8]{...) while((s32[]{:T(128)}, f32[8,128]{1,0:T(8,128)S(1)}, ...), condition=%wide.region_25.27_spmd, body=%wide.region_22.26_spmd.sunk | while | flops 15470 | bytes 19595 | solution.py:68
  790.1 42.5 %while.151 = (s32[]{:T(128)}, f32[128,4096]{1,0:T(8,128)S(1)}, f32[8,128]{1,0:T(8,128)S(1)}, f32[]{:T(128)}, f32[8]{0:T(128)S(1)}, /*index=5*/f32[8]{0:T(128)S(1...) while((s32[]{:T(128)}, f32[128,4096]{1,0:T(8,128)S(1)}, ...), condition=%wide.region_27.29_spmd.clone, body=%wide.region_26.28_spmd.clone.sunk | while | flops 7450626 | bytes 6359205 | solution.py:86
  832.9 57.6 %all_to_all.33 = f32[1,128,32,128]{3,2,0,1:T(8,128)S(1)} all-to-all(f32[1,128,32,128]{3,2,0,1:T(8,128)S(1)} %bitcast.428), channel_id=1, replica_groups=mesh['lev'=4,'var'=64] {'var'}, dimensions={1} | all-to-all | bytes 4194304 | tf_op jit(solution)/shard_map/all_to_all | solution.py:151
  (686 shorter events, 331.8 us)
Async XLA Ops:
  5.5 13.3 %copy-start = (s32[4,8]{1,0:T(4,128)S(1)}, s32[4,8]{1,0:T(4,128)}, u32[]{:S(2)}) copy-start(s32[4,8]{1,0:T(4,128)} %param.33) | copy-start | bytes 388
  5.5 13.4 %copy-start.2 = (s32[4,64]{1,0:T(4,128)S(1)}, s32[4,64]{1,0:T(4,128)}, u32[]{:S(2)}) copy-start(s32[4,64]{1,0:T(4,128)} %param.35) | copy-start | bytes 3076
  5.5 13.4 %copy-start.1 = (s32[4]{0:T(128)S(1)}, s32[4]{0:T(128)}, u32[]{:S(2)}) copy-start(s32[4]{0:T(128)} %param.34) | copy-start | bytes 52
  5.5 64.5 %all-to-all-start = ((f32[1,2,2048,128]{3,1,0,2:T(2,128)}), f32[1,2,2048,128]{3,1,0,2:T(2,128)S(1)}, u32[]{:S(2)}, u32[]{:S(2)}) async-start(f32[1,2,2048,128]{3,1,0,2:T(2,128)} %copy.23), calls=%async_computation | async-start | bytes 4194304 | tf_op jit(solution)/shard_map/all_to_all | solution.py:100
  18.8 12.6 %copy-start.3 = (f32[4,8]{1,0:T(4,128)S(1)}, f32[4,8]{1,0:T(4,128)}, u32[]{:S(2)}) copy-start(f32[4,8]{1,0:T(4,128)} %param.36) | copy-start | bytes 388
  18.8 12.6 %copy-start.4 = (f32[4,8]{1,0:T(4,128)S(1)}, f32[4,8]{1,0:T(4,128)}, u32[]{:S(2)}) copy-start(f32[4,8]{1,0:T(4,128)} %param.37) | copy-start | bytes 388
where the time goes:
time: 896 us; the launch traced here: 892 us
  blocking collectives  354 us (40%)
  local copies, waits for them, and re-layouts  168 us (19%)
  other arithmetic  123 us (14%)
  loops' own time  109 us (12%)
  matrix products  78.3 us (9%)
  waiting for transfers between devices  38.6 us (4%)
  starting transfers between devices  13.3 us (1%)
    psum x4, blocking collectives, from_root(): return lax.psum(jnp.where(mine, array, jnp.zeros_like(array)), axis)  296 us
    another operation x4, loops' own time, assimilate(): lax.fori_loop(0, count, assimilate_one_obs, (priors, empty, empty, jnp.ze...  108 us
    div x32, other arithmetic, serial_one_obs(): weight * regress / scales[obs_index]  61.1 us
    all_to_all x1, blocking collectives, shards(): lax.all_to_all(field.reshape(1, members, tile_width, y_all), 'var', split...  57.6 us
    dot_general x32, matrix products, assimilate_one_obs(): regress = jnp.dot(priors, anomaly, precision=lax.Precision.HIGHEST)  43.3 us
    all_to_all x1, waiting for transfers between devices, shards(): lax.all_to_all(ensemble, 'var', split_axis=2, concat_axis=1, tiled=True)  38.6 us
    dot_general x32, matrix products, serial_one_obs(): jnp.dot(anomalies[obs_index], field, precision=lax.Precision.HIGHEST)  35.1 us
    dynamic_slice x32, local copies, waits for them, and re-layouts, assimilate_one_obs(): values[obs_index]  20.3 us
  transfers between devices with their start and end apart: 1, of which 1 were waited for; matrix products, arithmetic and copies ran while one was open for 1% of the time, Pallas kernels for 0%

commit v1 on v0

v1 whole, which is shorter than its diff:
```python
import functools

import jax
import jax.numpy as jnp
from jax import lax
from jax.experimental import pallas as pl
from jax.experimental.pallas import tpu as pltpu
from jax.sharding import PartitionSpec as P

MESH = pl.DeviceIdType.MESH
HIGHEST = lax.Precision.HIGHEST
F32 = jnp.float32
REACH = 3
HALF = 64


def step_at(value, edge):
    return jnp.minimum(jnp.maximum(value - edge + 1, 0), 1)


def changed_tiles(owner_ref, blocks, tiles, slots):
    t = [owner_ref[b] & (tiles - 1) for b in range(blocks)]
    for i in range(blocks):
        for j in range(blocks - 1 - i):
            t[j], t[j + 1] = jnp.minimum(t[j], t[j + 1]), jnp.maximum(t[j], t[j + 1])
    befores, gaps, total, end = [], [], 0, -1
    for b in range(blocks):
        start = jnp.maximum(jnp.maximum(t[b] - REACH, end + 1), 0)
        gaps.append(start - end - 1)
        end = jnp.minimum(t[b] + REACH, tiles - 1)
        befores.append(total)
        total = total + jnp.maximum(end - start + 1, 0)
    found = []
    for s in range(slots):
        tile = gaps[0] + s
        for b in range(1, blocks):
            tile = tile + gaps[b] * step_at(s, befores[b])
        found.append((tile + 1) * step_at(total - 1, s) - 1)
    return found


def taper(dx, dy, radius):
    return jnp.square(jnp.maximum(0.0, 1.0 - (dx * dx + dy * dy) / (radius * radius)))


def exchange_kernel(
    cfg,
    sites_ref,
    owner_ref,
    values_ref,
    errors_ref,
    ens_ref,
    back_ref,
    ens_v,
    out_buf,
    in_buf,
    ret_buf,
    site_v,
    near_buf,
    row_buf,
    row_in,
    wcol_v,
    wcell_v,
    hcol_v,
    r_v,
    load_sem,
    near_send,
    near_recv,
    row_send,
    row_recv,
    bulk_send,
    bulk_recv,
    ret_send,
    ret_recv,
    own_sem,
):
    levels, count, slots, tiles, width, blocks, obs = cfg
    n_obs = blocks * obs
    members = 2 * count
    lev = lax.axis_index("lev")
    me = lax.axis_index("var")
    radius = jnp.float32(REACH * width)
    tile_bits = tiles.bit_length() - 1

    barrier = pltpu.get_barrier_semaphore()

    def greet(j, carry):
        pl.semaphore_signal(
            barrier, inc=1, device_id=(lev, (me + j) % count), device_id_type=MESH
        )
        return carry

    lax.fori_loop(1, count, greet, 0)
    for j in range(1, levels):
        pl.semaphore_signal(
            barrier, inc=1, device_id=((lev + j) % levels, me), device_id_type=MESH
        )

    load = pltpu.make_async_copy(ens_ref, ens_v, load_sem)
    load.start()

    lane = lax.broadcasted_iota(jnp.int32, (1, 128), 1)
    low = lane < HALF
    tile_at = changed_tiles(owner_ref, blocks, tiles, slots)

    sub32 = lax.broadcasted_iota(jnp.int32, (n_obs, 128), 0)
    lane32 = lax.broadcasted_iota(jnp.int32, (n_obs, 128), 1)
    site_c = jnp.zeros((n_obs, 128), jnp.int32)
    own_c = jnp.zeros((n_obs, 128), jnp.int32)
    err_c = jnp.zeros((n_obs, 128), F32)
    val_c = jnp.zeros((n_obs, 128), F32)
    site_r = jnp.zeros((1, 128), jnp.int32)
    own_r = jnp.zeros((1, 128), jnp.int32)
    for i in range(n_obs):
        b, k = i // obs, i % obs
        at = sub32 == i
        site_c = jnp.where(at, sites_ref[b, k], site_c)
        own_c = jnp.where(at, owner_ref[b], own_c)
        err_c = jnp.where(at, errors_ref[b, k], err_c)
        val_c = jnp.where(at, values_ref[b, k], val_c)
        site_r = jnp.where(lane == i, sites_ref[b, k], site_r)
        own_r = jnp.where(lane == i, owner_ref[b], own_r)
    x_c = (site_c >> 7).astype(F32)
    y_c = (site_c & 127).astype(F32)
    t_c = own_c & (tiles - 1)
    l_c = own_c >> tile_bits
    x_r = (site_r >> 7).astype(F32)
    y_r = (site_r & 127).astype(F32)
    t_r = own_r & (tiles - 1)
    l_r = own_r >> tile_bits
    pair_w = (
        jnp.where(jnp.abs(t_c - t_r) <= REACH, 1.0, 0.0)
        * jnp.exp2(-jnp.abs(l_c - l_r).astype(F32))
        * taper(x_c - x_r, y_c - y_r, radius)
    )
    row_w = jnp.where((lane32 > sub32) & (lane32 < n_obs), pair_w, 0.0)
    for k in range(n_obs):
        b = k // obs
        site = sites_ref[b, k % obs]
        own = owner_ref[b]
        w = (
            jnp.where(jnp.abs(t_c - (own & (tiles - 1))) <= REACH, 1.0, 0.0)
            * jnp.exp2(-jnp.abs(l_c - (own >> tile_bits)).astype(F32))
            * taper(x_c - (site >> 7).astype(F32), y_c - (site & 127).astype(F32), radius)
        )
        wcol_v[k] = jnp.where(sub32 > k, w, 0.0)

    group, side, column = me // 16, (me // 8) % 2, me % 8
    cell_y = (side * HALF + lane % HALF).astype(F32)
    level_f = jnp.exp2(-jnp.abs(l_c - lev).astype(F32))
    for p in range(slots // 2):
        tile = jnp.where(low, tile_at[2 * p], tile_at[2 * p + 1])
        cell_x = (tile * width + group * 8 + column).astype(F32)
        inside = (tile >= 0) & (jnp.abs(t_c - tile) <= REACH)
        wcell_v[p] = (
            jnp.where(inside, 1.0, 0.0) * level_f * taper(cell_x - x_c, cell_y - y_c, radius)
        )

    load.wait()

    for m in range(2):
        for i in range(n_obs):
            b, k = i // obs, i % obs
            site = sites_ref[b, k]
            away = (owner_ref[b] >> tile_bits) - lev
            row = ens_v[m, site >> 10, pl.ds((site >> 7) & 7, 1), :]
            site_v[pl.ds(m * n_obs + i, 1), :] = jnp.where(
                lane == (site & 127) + 128 * away, row, 0.0
            )
    sums = jnp.sum(site_v[...], axis=1, keepdims=True)
    sub64 = lax.broadcasted_iota(jnp.int32, (2 * n_obs, 128), 0)
    lane64 = lax.broadcasted_iota(jnp.int32, (2 * n_obs, 128), 1)
    mine = jnp.sum(jnp.where(sub64 == lane64, sums, 0.0), axis=0, keepdims=True)
    near_buf[pl.ds(0, 8), :] = jnp.broadcast_to(mine, (8, 128))

    for s in range(slots):
        tile = jnp.maximum(tile_at[s], 0)
        for g in range(4):
            a = ens_v[0, tile * (width // 8) + g]
            c = ens_v[1, tile * (width // 8) + g]
            out_buf[pl.ds((g * 16) * slots + s, 8, stride=slots), :] = jnp.where(
                low, a, pltpu.roll(c, HALF, 1)
            )
            out_buf[pl.ds((g * 16 + 8) * slots + s, 8, stride=slots), :] = jnp.where(
                low, pltpu.roll(a, HALF, 1), c
            )

    pl.semaphore_wait(barrier, count - 1 + levels - 1)

    near = []
    for j in range(1, levels):
        copy = pltpu.make_async_remote_copy(
            near_buf.at[pl.ds(0, 8)],
            near_buf.at[pl.ds(8 * j, 8)],
            near_send.at[j],
            near_recv.at[j],
            device_id=((lev + j) % levels, me),
            device_id_type=MESH,
        )
        copy.start()
        near.append(copy)

    def send_out(j, carry):
        to = (me + j) % count
        pltpu.make_async_remote_copy(
            out_buf.at[pl.ds(to * slots, slots)],
            in_buf.at[pl.ds(me * slots, slots)],
            bulk_send,
            bulk_recv,
            device_id=(lev, to),
            device_id_type=MESH,
        ).start()
        return carry

    for copy in near:
        copy.wait_recv()
    row_buf[...] = (near_buf[pl.ds(0, 8), :] + near_buf[pl.ds(8, 8), :]) + (
        near_buf[pl.ds(16, 8), :] + near_buf[pl.ds(24, 8), :]
    )

    def send_row(j, carry):
        to = (me + j) % count
        pltpu.make_async_remote_copy(
            row_buf.at[pl.ds(0, 1)],
            row_in.at[pl.ds(me, 1)],
            row_send,
            row_recv,
            device_id=(lev, to),
            device_id_type=MESH,
        ).start()
        return carry

    lax.fori_loop(1, count, send_row, 0)
    lax.fori_loop(1, count, send_out, 0)
    row_in[pl.ds(me, 1), :] = row_buf[pl.ds(0, 1), :]
    in_buf[pl.ds(me * slots, slots), :] = out_buf[pl.ds(me * slots, slots), :]
    for copy in near:
        copy.wait_send()
    pltpu.make_async_copy(
        row_in.at[pl.ds(0, count - 1)], row_in.at[pl.ds(0, count - 1)], row_recv
    ).wait()

    raw = row_in[...]
    total = jnp.sum(raw, axis=0, keepdims=True)
    both = jnp.where(lane < n_obs, total + pltpu.roll(total, 128 - n_obs, 1), 0.0)
    mean_r = both / members
    mean2_r = mean_r + pltpu.roll(mean_r, n_obs, 1)
    centred = jnp.where(lane < 2 * n_obs, raw - mean2_r, 0.0)
    full = lax.dot_general(
        centred, centred, (((0,), (0,)), ((), ())), precision=HIGHEST, preferred_element_type=F32
    )
    gram = full[:n_obs] + pltpu.roll(full[n_obs : 2 * n_obs], 128 - n_obs, 1)
    gram = jnp.where(lane < n_obs, gram, 0.0)
    mean_c = jnp.sum(jnp.where(sub32 == lane32, mean_r, 0.0), axis=1, keepdims=True)
    mean_c = jnp.broadcast_to(mean_c, (n_obs, 128))
    mix = jnp.where(sub32 == lane32, 1.0, 0.0)
    alpha_c = jnp.zeros((n_obs, 128), F32)
    beta_c = jnp.zeros((n_obs, 128), F32)
    inv_c = jnp.zeros((n_obs, 128), F32)
    beta_r = jnp.zeros((1, 128), F32)
    for k in range(n_obs):
        u_row = gram[k : k + 1, :]
        u_col = jnp.broadcast_to(gram[:, k : k + 1], (n_obs, 128))
        d = u_col[k : k + 1, :]
        spread = d / (members - 1) + 1e-06
        r = err_c[k : k + 1, :]
        inv = 1.0 / (spread + r)
        alpha = spread * inv * (val_c[k : k + 1, :] - mean_c[k : k + 1, :])
        beta = jnp.sqrt(r * inv) - 1.0
        inv_scaled = 1.0 / ((members - 1) * spread)
        c_col = wcol_v[k] * u_col * inv_scaled
        g_row = row_w[k : k + 1, :] * u_row * (inv_scaled * beta)
        g_col = c_col * beta
        mean_c = mean_c + c_col * alpha
        gram = gram + (g_col * (u_row + g_row * d) + u_col * g_row)
        mix = mix + g_col * mix[k : k + 1, :]
        at = sub32 == k
        alpha_c = jnp.where(at, alpha, alpha_c)
        beta_c = jnp.where(at, beta, beta_c)
        inv_c = jnp.where(at, inv_scaled, inv_c)
        beta_r = jnp.where(lane == k, beta, beta_r)
    lower = jnp.where(lane32 < sub32, gram * beta_r, 0.0)
    for k in range(n_obs):
        hcol_v[k] = jnp.broadcast_to(lower[:, k : k + 1], (n_obs, 128))

    mix2 = jnp.concatenate([mix, pltpu.roll(mix, n_obs, 1)], axis=0)
    anomalies = lax.dot_general(
        mix2, centred, (((1,), (1,)), ((), ())), precision=HIGHEST, preferred_element_type=F32
    )
    shift = (
        jnp.concatenate([alpha_c, alpha_c], axis=0)[:, :count]
        + jnp.concatenate([beta_c, beta_c], axis=0)[:, :count] * anomalies
    )

    pltpu.make_async_copy(
        in_buf.at[pl.ds(0, (count - 1) * slots)],
        in_buf.at[pl.ds(0, (count - 1) * slots)],
        bulk_recv,
    ).wait()

    def half_sum(part):
        t = jnp.where(low, part[:n_obs], part[n_obs:])
        return t + pltpu.roll(t, HALF, 1)

    for p in range(slots // 2):
        x = jnp.concatenate(
            [
                in_buf[pl.ds(2 * p, count, stride=slots), :],
                in_buf[pl.ds(2 * p + 1, count, stride=slots), :],
            ],
            axis=1,
        )
        r2 = jnp.dot(anomalies, x, precision=HIGHEST, preferred_element_type=F32)
        r_v[p] = jnp.where(low, half_sum(r2[:, :128]), half_sum(r2[:, 128:]))

    for p in range(slots // 2):
        reg = r_v[p]
        w = wcell_v[p] * inv_c
        rows = []
        for k in range(n_obs):
            coef = w[k : k + 1, :] * reg[k : k + 1, :]
            rows.append(coef)
            if k + 1 < n_obs:
                reg = reg + hcol_v[k] * coef
        coefs = w * reg
        turned = pltpu.roll(coefs, HALF, 1)
        zero = jnp.zeros_like(coefs)
        first = jnp.concatenate(
            [jnp.where(low, coefs, zero), jnp.where(low, zero, turned)], axis=0
        )
        second = jnp.concatenate(
            [jnp.where(low, turned, zero), jnp.where(low, zero, coefs)], axis=0
        )
        delta = lax.dot_general(
            shift,
            jnp.concatenate([first, second], axis=1),
            (((0,), (0,)), ((), ())),
            precision=HIGHEST,
            preferred_element_type=F32,
        )
        ret_buf[pl.ds(2 * p, count, stride=slots), :] = delta[:, :128]
        ret_buf[pl.ds(2 * p + 1, count, stride=slots), :] = delta[:, 128:]

    def send_back(j, carry):
        to = (me + j) % count
        pltpu.make_async_remote_copy(
            ret_buf.at[pl.ds(to * slots, slots)],
            back_ref.at[pl.ds(me * slots, slots)],
            ret_send,
            ret_recv,
            device_id=(lev, to),
            device_id_type=MESH,
        ).start()
        return carry

    lax.fori_loop(1, count, send_back, 0)
    own = pltpu.make_async_copy(
        ret_buf.at[pl.ds(me * slots, slots)], back_ref.at[pl.ds(me * slots, slots)], own_sem
    )
    own.start()
    rest = pl.ds(0, (count - 1) * slots)
    pltpu.make_async_copy(row_in.at[pl.ds(0, count - 1)], row_in.at[pl.ds(0, count - 1)], row_send).wait()
    pltpu.make_async_copy(out_buf.at[rest], out_buf.at[rest], bulk_send).wait()
    own.wait()
    pltpu.make_async_copy(back_ref.at[rest], back_ref.at[rest], ret_recv).wait()
    pltpu.make_async_copy(ret_buf.at[rest], ret_buf.at[rest], ret_send).wait()


def apply_kernel(cfg, owner_ref, ens_ref, back_ref, out_ref, ens_v, back_v, sems):
    levels, count, slots, tiles, width, blocks, obs = cfg
    load = pltpu.make_async_copy(ens_ref, ens_v, sems.at[0])
    load_back = pltpu.make_async_copy(back_ref, back_v, sems.at[1])
    load_back.start()
    load.start()
    tile_at = changed_tiles(owner_ref, blocks, tiles, slots)
    low = lax.broadcasted_iota(jnp.int32, (1, 128), 1) < HALF
    load_back.wait()
    load.wait()
    for s in range(slots):
        tile = jnp.maximum(tile_at[s], 0)
        for g in range(4):
            a = back_v[pl.ds((g * 16) * slots + s, 8, stride=slots), :]
            c = back_v[pl.ds((g * 16 + 8) * slots + s, 8, stride=slots), :]
            at = tile * (width // 8) + g
            ens_v[0, at] = ens_v[0, at] + jnp.where(low, a, pltpu.roll(c, HALF, 1))
            ens_v[1, at] = ens_v[1, at] + jnp.where(low, pltpu.roll(a, HALF, 1), c)
    store = pltpu.make_async_copy(ens_v, out_ref, sems.at[2])
    store.start()
    store.wait()


def shards(slots, ensemble, obs_sites, owner, tile_mask, obs_values, obs_error):
    levels, count = lax.axis_size("lev"), lax.axis_size("var")
    _, m_dev, x_all, y_all = ensemble.shape
    tiles = tile_mask.shape[1]
    width = x_all // tiles
    blocks, obs = obs_sites.shape
    n_obs = blocks * obs
    cfg = (levels, count, slots, tiles, width, blocks, obs)
    ens = ensemble.reshape(m_dev, x_all // 8, 8, y_all)
    smem = pl.BlockSpec(memory_space=pltpu.SMEM)
    anywhere = pl.BlockSpec(memory_space=pl.ANY)
    dma = pltpu.SemaphoreType.DMA
    back = pl.pallas_call(
        functools.partial(exchange_kernel, cfg),
        out_shape=jax.ShapeDtypeStruct((count * slots, 128), F32),
        in_specs=[smem] * 4 + [anywhere],
        out_specs=anywhere,
        scratch_shapes=[
            pltpu.VMEM(ens.shape, F32),
            pltpu.VMEM((count * slots, 128), F32),
            pltpu.VMEM((count * slots, 128), F32),
            pltpu.VMEM((count * slots, 128), F32),
            pltpu.VMEM((2 * n_obs, 128), F32),
            pltpu.VMEM((8 * levels, 128), F32),
            pltpu.VMEM((8, 128), F32),
            pltpu.VMEM((count, 128), F32),
            pltpu.VMEM((n_obs, n_obs, 128), F32),
            pltpu.VMEM((slots // 2, n_obs, 128), F32),
            pltpu.VMEM((n_obs, n_obs, 128), F32),
            pltpu.VMEM((slots // 2, n_obs, 128), F32),
            dma,
            dma((levels,)),
            dma((levels,)),
            dma,
            dma,
            dma,
            dma,
            dma,
            dma,
            dma,
        ],
        compiler_params=pltpu.CompilerParams(
            collective_id=slots, has_side_effects=True, vmem_limit_bytes=40 * 2**20
        ),
    )(obs_sites, owner, obs_values, obs_error, ens)
    out = pl.pallas_call(
        functools.partial(apply_kernel, cfg),
        out_shape=jax.ShapeDtypeStruct(ens.shape, F32),
        in_specs=[smem, anywhere, anywhere],
        out_specs=anywhere,
        scratch_shapes=[
            pltpu.VMEM(ens.shape, F32),
            pltpu.VMEM((count * slots, 128), F32),
            dma((3,)),
        ],
        compiler_params=pltpu.CompilerParams(vmem_limit_bytes=40 * 2**20),
    )(owner, ens, back)
    return out.reshape(ensemble.shape)


def solution(mesh):
    in_specs = (P("lev", "var", None, None), P(), P(), P(), P(), P())
    out_specs = P("lev", "var", None, None)
    return jax.shard_map(
        functools.partial(shards, 32),
        mesh=mesh,
        in_specs=in_specs,
        out_specs=out_specs,
        check_vma=False,
    )
```

time: 896 us -> 78.7 us (0.09)
  blocking collectives: 354 us -> 0 us
  local copies, waits for them, and re-layouts: 168 us -> 4.29 us
  other arithmetic: 123 us -> 0 us
  loops' own time: 109 us -> 0 us
  matrix products: 78.3 us -> 0 us
  Pallas kernels: 0 us -> 74.1 us
  waiting for transfers between devices: 38.6 us -> 0 us
  starting transfers between devices: 13.3 us -> 0 us
    psum x4 -> x0, blocking collectives: 296 us -> none  [from_root(): return lax.psum(jnp.where(mine, array, jnp.zeros_like(array)), axis)]
    dynamic_slice x225 -> x0, local copies, waits for them, and re-layouts: 137 us -> none  [the longest x32 20.3 us: assimilate_one_obs(): values[obs_index]]
    another operation x8 -> x0, loops' own time: 109 us -> none  [the longest x4 108 us: assimilate(): lax.fori_loop(0, count, assimilate_one_obs, (priors, empty, empty, jnp.ze...]
    dot_general x64 -> x0, matrix products: 78.3 us -> none  [the longest x32 43.3 us: assimilate_one_obs(): regress = jnp.dot(priors, anomaly, precision=lax.Precision.HIGHEST)]
    pallas_call x0 -> x2, Pallas kernels: none -> 74.1 us  [the longest x1 70.7 us: shards(): pl.pallas_call(functools.partial(exchange_kernel, cfg), out_shape=jax.Sha...]
    div x32 -> x0, other arithmetic: 61.1 us -> none  [serial_one_obs(): weight * regress / scales[obs_index]]
    all_to_all x1 -> x0, blocking collectives: 57.6 us -> none  [shards(): lax.all_to_all(field.reshape(1, members, tile_width, y_all), 'var', split...]
    reduce_sum x64 -> x0, other arithmetic: 38.9 us -> none  [the longest x32 19.5 us: obs_increment(): spread = jnp.sum(anomaly * anomaly) / (members - 1) + 1e-06]
  transfers between devices with their start and end apart: 1 -> 0, of which waited for: 1 -> 0; matrix products, arithmetic and copies ran while one was open for 1% -> 0% of each run, Pallas kernels for 0% -> 0%
where the time goes in v1:
time: 78.7 us; the launch traced here: 78.4 us
  Pallas kernels  74.1 us (94%)
  local copies, waits for them, and re-layouts  4.29 us (5%)
    pallas_call x1, Pallas kernels, shards(): pl.pallas_call(functools.partial(exchange_kernel, cfg), out_shape=jax.Sha...  70.7 us
    unnamed x12, local copies, waits for them, and re-layouts  4.29 us
    pallas_call x1, Pallas kernels, shards(): pl.pallas_call(functools.partial(apply_kernel, cfg), out_shape=jax.ShapeD...  3.36 us

profile of v1, /device:TPU:1, one launch (start us, length us, event | category | flops | bytes accessed | tf_op | source)
XLA Modules:
  0.0 78.4 jit_solution(10928490356254356022)
XLA Ops:
  0.0 0.0 copy-start
  0.0 1.6 %copy-done = f32[1,2,2048,128]{3,2,1,0:T(8,128)S(1)} copy-done((f32[1,2,2048,128]{3,2,1,0:T(8,128)S(1)}, f32[1,2,2048,128]{3,2,1,0:T(8,128)}, u32[]{:S(2)}) %copy-start) | copy-done | bytes 2097176
  1.6 0.0 copy-start.2
  1.6 0.7 copy-done.2
  2.3 0.0 copy-start.3
  2.3 0.7 copy-done.3
  3.0 0.0 copy-start.4
  3.0 0.7 copy-done.4
  3.6 0.0 copy-start.5
  3.6 0.7 copy-done.5
  4.3 0.0 copy-start.1
  4.3 70.7 %shard_map.55.back_ref = f32[2048,128]{1,0:T(8,128)S(1)} custom-call(s32[4,8]{1,0:T(4,128)S(1)} %copy-done.2, s32[4]{0:T(128)S(1)} %copy-done.5, f32[4,8]{1,0:T(4,128)S(1)} %copy-done.3, f32[4,8]{1,0:T(4,128)S(1)} %copy-done.4, f32[2,256,8,128]{3,2,1,0:T(8,128)S(1)} %bitcast.2), custom_call_target="tpu_custom_call" | custom-call | tf_op jit(solution)/shard_map/pallas_call | solution.py:404
  75.0 0.0 copy-done.1
  75.0 3.4 %shard_map.56 = f32[2,256,8,128]{3,2,1,0:T(8,128)} custom-call(s32[4]{0:T(128)S(1)} %copy-done.5, f32[2,256,8,128]{3,2,1,0:T(8,128)S(1)} %bitcast.3, f32[2048,128]{1,0:T(8,128)S(1)} %shard_map.55.back_ref), custom_call_target="tpu_custom_call" | custom-call | tf_op jit(solution)/shard_map/pallas_call | solution.py:437
Async XLA Ops:
  0.0 1.6 %copy-start = (f32[1,2,2048,128]{3,2,1,0:T(8,128)S(1)}, f32[1,2,2048,128]{3,2,1,0:T(8,128)}, u32[]{:S(2)}) copy-start(f32[1,2,2048,128]{3,2,1,0:T(8,128)} %param.6) | copy-start | bytes 6291460
  1.6 0.7 copy-start.2
  2.3 0.7 copy-start.3
  3.0 0.7 copy-start.4
  3.6 0.7 copy-start.5
  4.3 70.7 %copy-start.1 = (f32[1,2,2048,128]{3,2,1,0:T(8,128)S(1)}, f32[1,2,2048,128]{3,2,1,0:T(8,128)}, u32[]{:S(2)}) copy-start(f32[1,2,2048,128]{3,2,1,0:T(8,128)} %param.6) | copy-start | bytes 6291460

commit v2 on v1

--- a/solution.py
+++ b/solution.py
@@ -11,6 +11,8 @@
 HIGHEST = lax.Precision.HIGHEST
 F32 = jnp.float32
 REACH = 3
+SIZES = (22, 28)
+VMEM_BYTES = 64 * 2**20
 HALF = 64
 
 
@@ -45,12 +47,16 @@
 
 def exchange_kernel(
     cfg,
+    sites_hbm,
+    owner_hbm,
+    values_hbm,
+    errors_hbm,
+    ens_ref,
+    back_ref,
     sites_ref,
     owner_ref,
     values_ref,
     errors_ref,
-    ens_ref,
-    back_ref,
     ens_v,
     out_buf,
     in_buf,
@@ -64,6 +70,7 @@
     hcol_v,
     r_v,
     load_sem,
+    small_sem,
     near_send,
     near_recv,
     row_send,
@@ -82,6 +89,22 @@
     radius = jnp.float32(REACH * width)
     tile_bits = tiles.bit_length() - 1
 
+    load = pltpu.make_async_copy(ens_ref, ens_v, load_sem)
+    small = [
+        pltpu.make_async_copy(src, dst, small_sem.at[i])
+        for i, (src, dst) in enumerate(
+            [
+                (owner_hbm, owner_ref),
+                (sites_hbm, sites_ref),
+                (values_hbm, values_ref),
+                (errors_hbm, errors_ref),
+            ]
+        )
+    ]
+    for copy in small:
+        copy.start()
+    load.start()
+
     barrier = pltpu.get_barrier_semaphore()
 
     def greet(j, carry):
@@ -96,8 +119,8 @@
             barrier, inc=1, device_id=((lev + j) % levels, me), device_id_type=MESH
         )
 
-    load = pltpu.make_async_copy(ens_ref, ens_v, load_sem)
-    load.start()
+    for copy in small:
+        copy.wait()
 
     lane = lax.broadcasted_iota(jnp.int32, (1, 128), 1)
     low = lane < HALF
@@ -366,47 +389,58 @@
     pltpu.make_async_copy(ret_buf.at[rest], ret_buf.at[rest], ret_send).wait()
 
 
-def apply_kernel(cfg, owner_ref, ens_ref, back_ref, out_ref, ens_v, back_v, sems):
+def apply_kernel(cfg, owner_hbm, ens_ref, back_ref, out_ref, owner_ref, ens_v, back_v, sems):
     levels, count, slots, tiles, width, blocks, obs = cfg
-    load = pltpu.make_async_copy(ens_ref, ens_v, sems.at[0])
+    small = pltpu.make_async_copy(owner_hbm, owner_ref, sems.at[0])
+    small.start()
     load_back = pltpu.make_async_copy(back_ref, back_v, sems.at[1])
     load_back.start()
-    load.start()
-    tile_at = changed_tiles(owner_ref, blocks, tiles, slots)
+    loads = [
+        pltpu.make_async_copy(ens_ref.at[m], ens_v.at[m], sems.at[2 + m]) for m in range(2)
+    ]
+    for load in loads:
+        load.start()
+    small.wait()
+    tile_at = [jnp.maximum(t, 0) for t in changed_tiles(owner_ref, blocks, tiles, slots)]
     low = lax.broadcasted_iota(jnp.int32, (1, 128), 1) < HALF
     load_back.wait()
-    load.wait()
-    for s in range(slots):
-        tile = jnp.maximum(tile_at[s], 0)
-        for g in range(4):
-            a = back_v[pl.ds((g * 16) * slots + s, 8, stride=slots), :]
-            c = back_v[pl.ds((g * 16 + 8) * slots + s, 8, stride=slots), :]
-            at = tile * (width // 8) + g
-            ens_v[0, at] = ens_v[0, at] + jnp.where(low, a, pltpu.roll(c, HALF, 1))
-            ens_v[1, at] = ens_v[1, at] + jnp.where(low, pltpu.roll(a, HALF, 1), c)
-    store = pltpu.make_async_copy(ens_v, out_ref, sems.at[2])
-    store.start()
-    store.wait()
-
-
-def shards(slots, ensemble, obs_sites, owner, tile_mask, obs_values, obs_error):
-    levels, count = lax.axis_size("lev"), lax.axis_size("var")
-    _, m_dev, x_all, y_all = ensemble.shape
-    tiles = tile_mask.shape[1]
-    width = x_all // tiles
-    blocks, obs = obs_sites.shape
+    stores = []
+    for m in range(2):
+        loads[m].wait()
+        for s in range(slots):
+            for g in range(4):
+                a = back_v[pl.ds((g * 16) * slots + s, 8, stride=slots), :]
+                c = back_v[pl.ds((g * 16 + 8) * slots + s, 8, stride=slots), :]
+                at = tile_at[s] * (width // 8) + g
+                if m == 0:
+                    added = jnp.where(low, a, pltpu.roll(c, HALF, 1))
+                else:
+                    added = jnp.where(low, pltpu.roll(a, HALF, 1), c)
+                ens_v[m, at] = ens_v[m, at] + added
+        store = pltpu.make_async_copy(ens_v.at[m], out_ref.at[m], sems.at[4 + m])
+        store.start()
+        stores.append(store)
+    for store in stores:
+        store.wait()
+
+
+def filter_tiles(cfg, ens, obs_sites, owner, obs_values, obs_error):
+    levels, count, slots, tiles, width, blocks, obs = cfg
     n_obs = blocks * obs
-    cfg = (levels, count, slots, tiles, width, blocks, obs)
-    ens = ensemble.reshape(m_dev, x_all // 8, 8, y_all)
-    smem = pl.BlockSpec(memory_space=pltpu.SMEM)
+    hbm = pl.BlockSpec(memory_space=pltpu.HBM)
     anywhere = pl.BlockSpec(memory_space=pl.ANY)
     dma = pltpu.SemaphoreType.DMA
+    limit = VMEM_BYTES - 4 * count * slots * 128
     back = pl.pallas_call(
         functools.partial(exchange_kernel, cfg),
         out_shape=jax.ShapeDtypeStruct((count * slots, 128), F32),
-        in_specs=[smem] * 4 + [anywhere],
+        in_specs=[hbm] * 5,
         out_specs=anywhere,
         scratch_shapes=[
+            pltpu.SMEM(obs_sites.shape, jnp.int32),
+            pltpu.SMEM(owner.shape, jnp.int32),
+            pltpu.SMEM(obs_values.shape, F32),
+            pltpu.SMEM(obs_error.shape, F32),
             pltpu.VMEM(ens.shape, F32),
             pltpu.VMEM((count * slots, 128), F32),
             pltpu.VMEM((count * slots, 128), F32),
@@ -420,6 +454,7 @@
             pltpu.VMEM((n_obs, n_obs, 128), F32),
             pltpu.VMEM((slots // 2, n_obs, 128), F32),
             dma,
+            dma((4,)),
             dma((levels,)),
             dma((levels,)),
             dma,
@@ -431,21 +466,41 @@
             dma,
         ],
         compiler_params=pltpu.CompilerParams(
-            collective_id=slots, has_side_effects=True, vmem_limit_bytes=40 * 2**20
+            collective_id=slots, has_side_effects=True, vmem_limit_bytes=limit
         ),
     )(obs_sites, owner, obs_values, obs_error, ens)
-    out = pl.pallas_call(
+    return pl.pallas_call(
         functools.partial(apply_kernel, cfg),
         out_shape=jax.ShapeDtypeStruct(ens.shape, F32),
-        in_specs=[smem, anywhere, anywhere],
-        out_specs=anywhere,
+        in_specs=[hbm, hbm, anywhere],
+        out_specs=hbm,
         scratch_shapes=[
+            pltpu.SMEM(owner.shape, jnp.int32),
             pltpu.VMEM(ens.shape, F32),
             pltpu.VMEM((count * slots, 128), F32),
-            dma((3,)),
+            dma((6,)),
         ],
-        compiler_params=pltpu.CompilerParams(vmem_limit_bytes=40 * 2**20),
+        compiler_params=pltpu.CompilerParams(vmem_limit_bytes=limit),
     )(owner, ens, back)
+
+
+def shards(sizes, ensemble, obs_sites, owner, tile_mask, obs_values, obs_error):
+    levels, count = lax.axis_size("lev"), lax.axis_size("var")
+    _, m_dev, x_all, y_all = ensemble.shape
+    blocks, obs = obs_sites.shape
+    tiles = tile_mask.shape[1]
+    ens = ensemble.reshape(m_dev, x_all // 8, 8, y_all)
+    rest = (ens, obs_sites, owner, obs_values, obs_error)
+    branches = [
+        functools.partial(filter_tiles, (levels, count, n, tiles, x_all // tiles, blocks, obs))
+        for n in sizes
+    ]
+    if len(sizes) == 1:
+        out = branches[0](*rest)
+    else:
+        touched = jnp.sum(jnp.max(tile_mask, axis=0))
+        which = sum((touched > n).astype(jnp.int32) for n in sizes[:-1])
+        out = lax.switch(which, branches, *rest)
     return out.reshape(ensemble.shape)
 
 
@@ -453,7 +508,7 @@
     in_specs = (P("lev", "var", None, None), P(), P(), P(), P(), P())
     out_specs = P("lev", "var", None, None)
     return jax.shard_map(
-        functools.partial(shards, 32),
+        functools.partial(shards, SIZES),
         mesh=mesh,
         in_specs=in_specs,
         out_specs=out_specs,

time: 78.7 us -> 60.7 us (0.77)
  Pallas kernels: 74.1 us -> 58.5 us
  local copies, waits for them, and re-layouts: 4.29 us -> 0.01 us
  other arithmetic: 0 us -> 1.33 us
    pallas_call x2, Pallas kernels: 74.1 us -> 58.5 us  [the longest x1 55.5 us: filter_tiles(): pl.pallas_call(functools.partial(exchange_kernel, cfg), out_shape=jax.Sha...]
    unnamed x12 -> x0, local copies, waits for them, and re-layouts: 4.29 us -> none
where the time goes in v2:
time: 60.7 us; the launch traced here: 60.6 us
  Pallas kernels  58.5 us (96%)
  other arithmetic  1.33 us (2%)
  between operations  0.66 us (1%)
    pallas_call x1, Pallas kernels, filter_tiles(): pl.pallas_call(functools.partial(exchange_kernel, cfg), out_shape=jax.Sha...  55.5 us
    pallas_call x1, Pallas kernels, filter_tiles(): pl.pallas_call(functools.partial(apply_kernel, cfg), out_shape=jax.ShapeD...  2.99 us

profile of v2, /device:TPU:1, one launch (start us, length us, event | category | flops | bytes accessed | tf_op | source)
XLA Modules:
  0.0 60.6 jit_solution(11116988383045399459)
XLA Ops:
  0.0 0.7 %reduce_max.9 = s32[64]{0:T(128)S(1)} reduce(s32[4,64]{1,0:T(4,128)} %param.11, s32[]{:T(128)} %constant.1.clone.1), dimensions={0}, to_apply=%region_0.0 | reduce | flops 192 | bytes 1284 | tf_op jit(solution)/shard_map/reduce_max | solution.py:501
  0.7 0.6 %reduce_sum.9 = s32[]{:T(128)} reduce(s32[64]{0:T(128)S(1)} %reduce_max.9, s32[]{:T(128)} %constant.0.clone.1), dimensions={0}, to_apply=%region_1.0 | reduce | flops 63 | bytes 264 | tf_op jit(solution)/shard_map/reduce_sum | solution.py:501
  2.0 58.6 %conditional.1 = (f32[1,2,2048,128]{3,2,1,0:T(8,128)}) conditional(s32[]{:T(128)} %clamp.3, (s32[4,8]{1,0:T(4,128)}, s32[4]{0:T(128)}, f32[4,8]{1,0:T(4,128)}, f32[4,8]{1,0:T(4,128)}, f32[2,256,8,128]{3,2,1,0:T(8,128)}) %tuple.18, (s32[4,8]{1,0:T(4,128)}, s32[4]{0:T(128)}, f32[4,8]{1,0:T(4,128)}, f32[4,8]{1,0:T(4,128)}, ...), branch_computations={%region_2.0_spmd, %region_3.0_spmd} | conditional | bytes 100 | solution.py:503
  2.0 0.0 copy-start
  2.0 55.5 %branch_0_fun.2.back_ref = f32[1408,128]{1,0:T(8,128)} custom-call(s32[4,8]{1,0:T(4,128)} %get-tuple-element.31.sites_hbm, s32[4]{0:T(128)} %get-tuple-element.29.owner_hbm, f32[4,8]{1,0:T(4,128)} %get-tuple-element.32.values_hbm, f32[4,8]{1,0:T(4,128)} %get-tuple-element.33.errors_hbm, f32[2,256,8,128]{3,2,1,0:T(8,128)} %get-tuple-element.30.ens_ref), custom_call_target="tpu_custom_call" | custom-call | tf_op jit(solution)/shard_map/cond/branch_0_fun/pallas_call | solution.py:434
  57.5 0.0 copy-done
  57.5 3.0 %branch_0_fun.3 = f32[2,256,8,128]{3,2,1,0:T(8,128)} custom-call(s32[4]{0:T(128)S(1)} %copy-done, f32[2,256,8,128]{3,2,1,0:T(8,128)} %get-tuple-element.30.ens_ref, f32[1408,128]{1,0:T(8,128)} %branch_0_fun.2.back_ref), custom_call_target="tpu_custom_call" | custom-call | tf_op jit(solution)/shard_map/cond/branch_0_fun/pallas_call | solution.py:472
Async XLA Ops:
  2.0 55.5 %copy-start = (s32[4]{0:T(128)S(1)}, s32[4]{0:T(128)}, u32[]{:S(2)}) copy-start(s32[4]{0:T(128)} %get-tuple-element.29.owner_hbm) | copy-start | bytes 52 | tf_op jit(solution)/shard_map/cond

commit v3 on v2

--- a/solution.py
+++ b/solution.py
@@ -12,6 +12,7 @@
 F32 = jnp.float32
 REACH = 3
 SIZES = (22, 28)
+EARLY = 32
 VMEM_BYTES = 64 * 2**20
 HALF = 64
 
@@ -109,7 +110,7 @@
 
     def greet(j, carry):
         pl.semaphore_signal(
-            barrier, inc=1, device_id=(lev, (me + j) % count), device_id_type=MESH
+            barrier, inc=1, device_id=(lev, lax.rem(me + j, count)), device_id_type=MESH
         )
         return carry
 
@@ -126,6 +127,85 @@
     low = lane < HALF
     tile_at = changed_tiles(owner_ref, blocks, tiles, slots)
 
+    load.wait()
+
+    for m in range(2):
+        for i in range(n_obs):
+            b, k = i // obs, i % obs
+            site = sites_ref[b, k]
+            away = (owner_ref[b] >> tile_bits) - lev
+            row = ens_v[m, site >> 10, pl.ds((site >> 7) & 7, 1), :]
+            site_v[pl.ds(m * n_obs + i, 1), :] = jnp.where(
+                lane == (site & 127) + 128 * away, row, 0.0
+            )
+    sums = jnp.sum(site_v[...], axis=1, keepdims=True)
+    sub64 = lax.broadcasted_iota(jnp.int32, (2 * n_obs, 128), 0)
+    lane64 = lax.broadcasted_iota(jnp.int32, (2 * n_obs, 128), 1)
+    mine = jnp.sum(jnp.where(sub64 == lane64, sums, 0.0), axis=0, keepdims=True)
+    near_buf[pl.ds(0, 8), :] = jnp.broadcast_to(mine, (8, 128))
+
+    for s in range(slots):
+        tile = jnp.maximum(tile_at[s], 0)
+        for g in range(4):
+            a = ens_v[0, tile * (width // 8) + g]
+            c = ens_v[1, tile * (width // 8) + g]
+            out_buf[pl.ds((g * 16) * slots + s, 8, stride=slots), :] = jnp.where(
+                low, a, pltpu.roll(c, HALF, 1)
+            )
+            out_buf[pl.ds((g * 16 + 8) * slots + s, 8, stride=slots), :] = jnp.where(
+                low, pltpu.roll(a, HALF, 1), c
+            )
+
+    pl.semaphore_wait(barrier, count - 1 + levels - 1)
+
+    near = []
+    for j in range(1, levels):
+        copy = pltpu.make_async_remote_copy(
+            near_buf.at[pl.ds(0, 8)],
+            near_buf.at[pl.ds(8 * j, 8)],
+            near_send.at[j],
+            near_recv.at[j],
+            device_id=((lev + j) % levels, me),
+            device_id_type=MESH,
+        )
+        copy.start()
+        near.append(copy)
+
+    def send_out(j, carry):
+        to = lax.rem(me + j, count)
+        pltpu.make_async_remote_copy(
+            out_buf.at[pl.ds(to * slots, slots)],
+            in_buf.at[pl.ds(me * slots, slots)],
+            bulk_send,
+            bulk_recv,
+            device_id=(lev, to),
+            device_id_type=MESH,
+        ).start()
+        return carry
+
+    lax.fori_loop(1, EARLY, send_out, 0)
+    for copy in near:
+        copy.wait_recv()
+    row_buf[...] = (near_buf[pl.ds(0, 8), :] + near_buf[pl.ds(8, 8), :]) + (
+        near_buf[pl.ds(16, 8), :] + near_buf[pl.ds(24, 8), :]
+    )
+
+    def send_row(j, carry):
+        to = lax.rem(me + j, count)
+        pltpu.make_async_remote_copy(
+            row_buf.at[pl.ds(0, 1)],
+            row_in.at[pl.ds(me, 1)],
+            row_send,
+            row_recv,
+            device_id=(lev, to),
+            device_id_type=MESH,
+        ).start()
+        return carry
+
+    lax.fori_loop(1, count, send_row, 0)
+    lax.fori_loop(EARLY, count, send_out, 0)
+    row_in[pl.ds(me, 1), :] = row_buf[pl.ds(0, 1), :]
+    in_buf[pl.ds(me * slots, slots), :] = out_buf[pl.ds(me * slots, slots), :]
     sub32 = lax.broadcasted_iota(jnp.int32, (n_obs, 128), 0)
     lane32 = lax.broadcasted_iota(jnp.int32, (n_obs, 128), 1)
     site_c = jnp.zeros((n_obs, 128), jnp.int32)
@@ -179,84 +259,6 @@
             jnp.where(inside, 1.0, 0.0) * level_f * taper(cell_x - x_c, cell_y - y_c, radius)
         )
 
-    load.wait()
-
-    for m in range(2):
-        for i in range(n_obs):
-            b, k = i // obs, i % obs
-            site = sites_ref[b, k]
-            away = (owner_ref[b] >> tile_bits) - lev
-            row = ens_v[m, site >> 10, pl.ds((site >> 7) & 7, 1), :]
-            site_v[pl.ds(m * n_obs + i, 1), :] = jnp.where(
-                lane == (site & 127) + 128 * away, row, 0.0
-            )
-    sums = jnp.sum(site_v[...], axis=1, keepdims=True)
-    sub64 = lax.broadcasted_iota(jnp.int32, (2 * n_obs, 128), 0)
-    lane64 = lax.broadcasted_iota(jnp.int32, (2 * n_obs, 128), 1)
-    mine = jnp.sum(jnp.where(sub64 == lane64, sums, 0.0), axis=0, keepdims=True)
-    near_buf[pl.ds(0, 8), :] = jnp.broadcast_to(mine, (8, 128))
-
-    for s in range(slots):
-        tile = jnp.maximum(tile_at[s], 0)
-        for g in range(4):
-            a = ens_v[0, tile * (width // 8) + g]
-            c = ens_v[1, tile * (width // 8) + g]
-            out_buf[pl.ds((g * 16) * slots + s, 8, stride=slots), :] = jnp.where(
-                low, a, pltpu.roll(c, HALF, 1)
-            )
-            out_buf[pl.ds((g * 16 + 8) * slots + s, 8, stride=slots), :] = jnp.where(
-                low, pltpu.roll(a, HALF, 1), c
-            )
-
-    pl.semaphore_wait(barrier, count - 1 + levels - 1)
-
-    near = []
-    for j in range(1, levels):
-        copy = pltpu.make_async_remote_copy(
-            near_buf.at[pl.ds(0, 8)],
-            near_buf.at[pl.ds(8 * j, 8)],
-            near_send.at[j],
-            near_recv.at[j],
-            device_id=((lev + j) % levels, me),
-            device_id_type=MESH,
-        )
-        copy.start()
-        near.append(copy)
-
-    def send_out(j, carry):
-        to = (me + j) % count
-        pltpu.make_async_remote_copy(
-            out_buf.at[pl.ds(to * slots, slots)],
-            in_buf.at[pl.ds(me * slots, slots)],
-            bulk_send,
-            bulk_recv,
-            device_id=(lev, to),
-            device_id_type=MESH,
-        ).start()
-        return carry
-
-    for copy in near:
-        copy.wait_recv()
-    row_buf[...] = (near_buf[pl.ds(0, 8), :] + near_buf[pl.ds(8, 8), :]) + (
-        near_buf[pl.ds(16, 8), :] + near_buf[pl.ds(24, 8), :]
-    )
-
-    def send_row(j, carry):
-        to = (me + j) % count
-        pltpu.make_async_remote_copy(
-            row_buf.at[pl.ds(0, 1)],
-            row_in.at[pl.ds(me, 1)],
-            row_send,
-            row_recv,
-            device_id=(lev, to),
-            device_id_type=MESH,
-        ).start()
-        return carry
-
-    lax.fori_loop(1, count, send_row, 0)
-    lax.fori_loop(1, count, send_out, 0)
-    row_in[pl.ds(me, 1), :] = row_buf[pl.ds(0, 1), :]
-    in_buf[pl.ds(me * slots, slots), :] = out_buf[pl.ds(me * slots, slots), :]
     for copy in near:
         copy.wait_send()
     pltpu.make_async_copy(
@@ -365,7 +367,7 @@
         ret_buf[pl.ds(2 * p + 1, count, stride=slots), :] = delta[:, 128:]
 
     def send_back(j, carry):
-        to = (me + j) % count
+        to = lax.rem(me + j, count)
         pltpu.make_async_remote_copy(
             ret_buf.at[pl.ds(to * slots, slots)],
             back_ref.at[pl.ds(me * slots, slots)],

time: 60.7 us -> 56.2 us (0.926)
  Pallas kernels: 58.5 us -> 54 us
    pallas_call x1, Pallas kernels: 55.5 us -> 51 us  [filter_tiles(): pl.pallas_call(functools.partial(exchange_kernel, cfg), out_shape=jax.Sha...]
where the time goes in v3:
time: 56.2 us; the launch traced here: 56 us
  Pallas kernels  54 us (96%)
  other arithmetic  1.33 us (2%)
  between operations  0.66 us (1%)
    pallas_call x1, Pallas kernels, filter_tiles(): pl.pallas_call(functools.partial(exchange_kernel, cfg), out_shape=jax.Sha...  51 us
    pallas_call x1, Pallas kernels, filter_tiles(): pl.pallas_call(functools.partial(apply_kernel, cfg), out_shape=jax.ShapeD...  3 us

profile of v3, /device:TPU:1, one launch (start us, length us, event | category | flops | bytes accessed | tf_op | source)
XLA Modules:
  0.0 56.0 jit_solution(17213955855157240681)
XLA Ops:
  0.0 0.7 %reduce_max.9 = s32[64]{0:T(128)S(1)} reduce(s32[4,64]{1,0:T(4,128)} %param.11, s32[]{:T(128)} %constant.1.clone.1), dimensions={0}, to_apply=%region_0.0 | reduce | flops 192 | bytes 1284 | tf_op jit(solution)/shard_map/reduce_max | solution.py:503
  0.7 0.6 %reduce_sum.9 = s32[]{:T(128)} reduce(s32[64]{0:T(128)S(1)} %reduce_max.9, s32[]{:T(128)} %constant.0.clone.1), dimensions={0}, to_apply=%region_1.0 | reduce | flops 63 | bytes 264 | tf_op jit(solution)/shard_map/reduce_sum | solution.py:503
  2.0 54.0 %conditional.1 = (f32[1,2,2048,128]{3,2,1,0:T(8,128)}) conditional(s32[]{:T(128)} %clamp.3, (s32[4,8]{1,0:T(4,128)}, s32[4]{0:T(128)}, f32[4,8]{1,0:T(4,128)}, f32[4,8]{1,0:T(4,128)}, f32[2,256,8,128]{3,2,1,0:T(8,128)}) %tuple.18, (s32[4,8]{1,0:T(4,128)}, s32[4]{0:T(128)}, f32[4,8]{1,0:T(4,128)}, f32[4,8]{1,0:T(4,128)}, ...), branch_computations={%region_2.0_spmd, %region_3.0_spmd} | conditional | bytes 100 | solution.py:505
  2.0 0.0 copy-start
  2.0 51.0 %branch_0_fun.2.back_ref = f32[1408,128]{1,0:T(8,128)} custom-call(s32[4,8]{1,0:T(4,128)} %get-tuple-element.31.sites_hbm, s32[4]{0:T(128)} %get-tuple-element.29.owner_hbm, f32[4,8]{1,0:T(4,128)} %get-tuple-element.32.values_hbm, f32[4,8]{1,0:T(4,128)} %get-tuple-element.33.errors_hbm, f32[2,256,8,128]{3,2,1,0:T(8,128)} %get-tuple-element.30.ens_ref), custom_call_target="tpu_custom_call" | custom-call | tf_op jit(solution)/shard_map/cond/branch_0_fun/pallas_call | solution.py:436
  53.0 0.0 copy-done
  53.0 3.0 %branch_0_fun.3 = f32[2,256,8,128]{3,2,1,0:T(8,128)} custom-call(s32[4]{0:T(128)S(1)} %copy-done, f32[2,256,8,128]{3,2,1,0:T(8,128)} %get-tuple-element.30.ens_ref, f32[1408,128]{1,0:T(8,128)} %branch_0_fun.2.back_ref), custom_call_target="tpu_custom_call" | custom-call | tf_op jit(solution)/shard_map/cond/branch_0_fun/pallas_call | solution.py:474
Async XLA Ops:
  2.0 51.0 %copy-start = (s32[4]{0:T(128)S(1)}, s32[4]{0:T(128)}, u32[]{:S(2)}) copy-start(s32[4]{0:T(128)} %get-tuple-element.29.owner_hbm) | copy-start | bytes 52 | tf_op jit(solution)/shard_map/cond

commit v4 on v3

--- a/solution.py
+++ b/solution.py
@@ -11,8 +11,7 @@
 HIGHEST = lax.Precision.HIGHEST
 F32 = jnp.float32
 REACH = 3
-SIZES = (22, 28)
-EARLY = 32
+LAYOUTS = ((8, 14), (10, 18))
 VMEM_BYTES = 64 * 2**20
 HALF = 64
 
@@ -40,6 +39,11 @@
             tile = tile + gaps[b] * step_at(s, befores[b])
         found.append((tile + 1) * step_at(total - 1, s) - 1)
     return found
+
+
+def places(parts, count):
+    firsts = [sum(parts[:p]) for p in range(len(parts))]
+    return firsts, [count * first for first in firsts]
 
 
 def taper(dx, dy, radius):
@@ -82,13 +86,15 @@
     ret_recv,
     own_sem,
 ):
-    levels, count, slots, tiles, width, blocks, obs = cfg
+    levels, count, parts, tiles, width, blocks, obs = cfg
+    slots = sum(parts)
     n_obs = blocks * obs
     members = 2 * count
     lev = lax.axis_index("lev")
     me = lax.axis_index("var")
     radius = jnp.float32(REACH * width)
     tile_bits = tiles.bit_length() - 1
+    firsts, bases = places(parts, count)
 
     load = pltpu.make_async_copy(ens_ref, ens_v, load_sem)
     small = [
@@ -144,17 +150,17 @@
     mine = jnp.sum(jnp.where(sub64 == lane64, sums, 0.0), axis=0, keepdims=True)
     near_buf[pl.ds(0, 8), :] = jnp.broadcast_to(mine, (8, 128))
 
-    for s in range(slots):
-        tile = jnp.maximum(tile_at[s], 0)
-        for g in range(4):
-            a = ens_v[0, tile * (width // 8) + g]
-            c = ens_v[1, tile * (width // 8) + g]
-            out_buf[pl.ds((g * 16) * slots + s, 8, stride=slots), :] = jnp.where(
-                low, a, pltpu.roll(c, HALF, 1)
-            )
-            out_buf[pl.ds((g * 16 + 8) * slots + s, 8, stride=slots), :] = jnp.where(
-                low, pltpu.roll(a, HALF, 1), c
-            )
+    for p, size in enumerate(parts):
+        for r in range(size):
+            tile = jnp.maximum(tile_at[firsts[p] + r], 0)
+            for g in range(4):
+                a = ens_v[0, tile * (width // 8) + g]
+                c = ens_v[1, tile * (width // 8) + g]
+                row = bases[p] + g * 16 * size + r
+                out_buf[pl.ds(row, 8, stride=size), :] = jnp.where(low, a, pltpu.roll(c, HALF, 1))
+                out_buf[pl.ds(row + 8 * size, 8, stride=size), :] = jnp.where(
+                    low, pltpu.roll(a, HALF, 1), c
+                )
 
     pl.semaphore_wait(barrier, count - 1 + levels - 1)
 
@@ -171,19 +177,28 @@
         copy.start()
         near.append(copy)
 
-    def send_out(j, carry):
-        to = lax.rem(me + j, count)
-        pltpu.make_async_remote_copy(
-            out_buf.at[pl.ds(to * slots, slots)],
-            in_buf.at[pl.ds(me * slots, slots)],
-            bulk_send,
-            bulk_recv,
-            device_id=(lev, to),
-            device_id_type=MESH,
-        ).start()
-        return carry
-
-    lax.fori_loop(1, EARLY, send_out, 0)
+    def send_part(p, src, dst, send_sem, recv_sem):
+        size = parts[p]
+
+        def send(j, carry):
+            to = lax.rem(me + j, count)
+            pltpu.make_async_remote_copy(
+                src.at[pl.ds(bases[p] + to * size, size)],
+                dst.at[pl.ds(bases[p] + me * size, size)],
+                send_sem.at[p],
+                recv_sem.at[p],
+                device_id=(lev, to),
+                device_id_type=MESH,
+            ).start()
+            return carry
+
+        lax.fori_loop(1, count, send, 0)
+
+    def wait_part(p, buf, sem):
+        rest = pl.ds(bases[p], (count - 1) * parts[p])
+        pltpu.make_async_copy(buf.at[rest], buf.at[rest], sem.at[p]).wait()
+
+    send_part(0, out_buf, in_buf, bulk_send, bulk_recv)
     for copy in near:
         copy.wait_recv()
     row_buf[...] = (near_buf[pl.ds(0, 8), :] + near_buf[pl.ds(8, 8), :]) + (
@@ -203,9 +218,12 @@
         return carry
 
     lax.fori_loop(1, count, send_row, 0)
-    lax.fori_loop(EARLY, count, send_out, 0)
+    for p in range(1, len(parts)):
+        send_part(p, out_buf, in_buf, bulk_send, bulk_recv)
     row_in[pl.ds(me, 1), :] = row_buf[pl.ds(0, 1), :]
-    in_buf[pl.ds(me * slots, slots), :] = out_buf[pl.ds(me * slots, slots), :]
+    for p, size in enumerate(parts):
+        here = pl.ds(bases[p] + me * size, size)
+        in_buf[here, :] = out_buf[here, :]
     sub32 = lax.broadcasted_iota(jnp.int32, (n_obs, 128), 0)
     lane32 = lax.broadcasted_iota(jnp.int32, (n_obs, 128), 1)
     site_c = jnp.zeros((n_obs, 128), jnp.int32)
@@ -317,84 +335,73 @@
         + jnp.concatenate([beta_c, beta_c], axis=0)[:, :count] * anomalies
     )
 
-    pltpu.make_async_copy(
-        in_buf.at[pl.ds(0, (count - 1) * slots)],
-        in_buf.at[pl.ds(0, (count - 1) * slots)],
-        bulk_recv,
-    ).wait()
-
     def half_sum(part):
         t = jnp.where(low, part[:n_obs], part[n_obs:])
         return t + pltpu.roll(t, HALF, 1)
 
-    for p in range(slots // 2):
-        x = jnp.concatenate(
-            [
-                in_buf[pl.ds(2 * p, count, stride=slots), :],
-                in_buf[pl.ds(2 * p + 1, count, stride=slots), :],
-            ],
-            axis=1,
-        )
-        r2 = jnp.dot(anomalies, x, precision=HIGHEST, preferred_element_type=F32)
-        r_v[p] = jnp.where(low, half_sum(r2[:, :128]), half_sum(r2[:, 128:]))
-
-    for p in range(slots // 2):
-        reg = r_v[p]
-        w = wcell_v[p] * inv_c
-        rows = []
-        for k in range(n_obs):
-            coef = w[k : k + 1, :] * reg[k : k + 1, :]
-            rows.append(coef)
-            if k + 1 < n_obs:
-                reg = reg + hcol_v[k] * coef
-        coefs = w * reg
-        turned = pltpu.roll(coefs, HALF, 1)
-        zero = jnp.zeros_like(coefs)
-        first = jnp.concatenate(
-            [jnp.where(low, coefs, zero), jnp.where(low, zero, turned)], axis=0
-        )
-        second = jnp.concatenate(
-            [jnp.where(low, turned, zero), jnp.where(low, zero, coefs)], axis=0
-        )
-        delta = lax.dot_general(
-            shift,
-            jnp.concatenate([first, second], axis=1),
-            (((0,), (0,)), ((), ())),
-            precision=HIGHEST,
-            preferred_element_type=F32,
-        )
-        ret_buf[pl.ds(2 * p, count, stride=slots), :] = delta[:, :128]
-        ret_buf[pl.ds(2 * p + 1, count, stride=slots), :] = delta[:, 128:]
-
-    def send_back(j, carry):
-        to = lax.rem(me + j, count)
-        pltpu.make_async_remote_copy(
-            ret_buf.at[pl.ds(to * slots, slots)],
-            back_ref.at[pl.ds(me * slots, slots)],
-            ret_send,
-            ret_recv,
-            device_id=(lev, to),
-            device_id_type=MESH,
-        ).start()
-        return carry
-
-    lax.fori_loop(1, count, send_back, 0)
-    own = pltpu.make_async_copy(
-        ret_buf.at[pl.ds(me * slots, slots)], back_ref.at[pl.ds(me * slots, slots)], own_sem
-    )
-    own.start()
-    rest = pl.ds(0, (count - 1) * slots)
-    pltpu.make_async_copy(row_in.at[pl.ds(0, count - 1)], row_in.at[pl.ds(0, count - 1)], row_send).wait()
-    pltpu.make_async_copy(out_buf.at[rest], out_buf.at[rest], bulk_send).wait()
-    own.wait()
-    pltpu.make_async_copy(back_ref.at[rest], back_ref.at[rest], ret_recv).wait()
-    pltpu.make_async_copy(ret_buf.at[rest], ret_buf.at[rest], ret_send).wait()
+    own = []
+    for p, size in enumerate(parts):
+        wait_part(p, in_buf, bulk_recv)
+        for q in range(size // 2):
+            row = bases[p] + 2 * q
+            x = jnp.concatenate(
+                [
+                    in_buf[pl.ds(row, count, stride=size), :],
+                    in_buf[pl.ds(row + 1, count, stride=size), :],
+                ],
+                axis=1,
+            )
+            r2 = jnp.dot(anomalies, x, precision=HIGHEST, preferred_element_type=F32)
+            r_v[firsts[p] // 2 + q] = jnp.where(low, half_sum(r2[:, :128]), half_sum(r2[:, 128:]))
+
+        for q in range(size // 2):
+            row = bases[p] + 2 * q
+            reg = r_v[firsts[p] // 2 + q]
+            w = wcell_v[firsts[p] // 2 + q] * inv_c
+            for k in range(n_obs - 1):
+                reg = reg + hcol_v[k] * (w[k : k + 1, :] * reg[k : k + 1, :])
+            coefs = w * reg
+            turned = pltpu.roll(coefs, HALF, 1)
+            zero = jnp.zeros_like(coefs)
+            first = jnp.concatenate(
+                [jnp.where(low, coefs, zero), jnp.where(low, zero, turned)], axis=0
+            )
+            second = jnp.concatenate(
+                [jnp.where(low, turned, zero), jnp.where(low, zero, coefs)], axis=0
+            )
+            delta = lax.dot_general(
+                shift,
+                jnp.concatenate([first, second], axis=1),
+                (((0,), (0,)), ((), ())),
+                precision=HIGHEST,
+                preferred_element_type=F32,
+            )
+            ret_buf[pl.ds(row, count, stride=size), :] = delta[:, :128]
+            ret_buf[pl.ds(row + 1, count, stride=size), :] = delta[:, 128:]
+
+        send_part(p, ret_buf, back_ref, ret_send, ret_recv)
+        here = pl.ds(bases[p] + me * size, size)
+        copy = pltpu.make_async_copy(ret_buf.at[here], back_ref.at[here], own_sem.at[p])
+        copy.start()
+        own.append(copy)
+
+    rows = row_in.at[pl.ds(0, count - 1)]
+    pltpu.make_async_copy(rows, rows, row_send).wait()
+    for p in range(len(parts)):
+        wait_part(p, out_buf, bulk_send)
+        own[p].wait()
+    for p in range(len(parts)):
+        wait_part(p, back_ref, ret_recv)
+    for p in range(len(parts)):
+        wait_part(p, ret_buf, ret_send)
 
 
 def apply_kernel(cfg, owner_hbm, ens_ref, back_ref, out_ref, owner_ref, ens_v, back_v, sems):
-    levels, count, slots, tiles, width, blocks, obs = cfg
+    levels, count, parts, tiles, width, blocks, obs = cfg
+    slots = sum(parts)
     small = pltpu.make_async_copy(owner_hbm, owner_ref, sems.at[0])
     small.start()
+    firsts, bases = places(parts, count)
     load_back = pltpu.make_async_copy(back_ref, back_v, sems.at[1])
     load_back.start()
     loads = [
@@ -409,16 +416,18 @@
     stores = []
     for m in range(2):
         loads[m].wait()
-        for s in range(slots):
-            for g in range(4):
-                a = back_v[pl.ds((g * 16) * slots + s, 8, stride=slots), :]
-                c = back_v[pl.ds((g * 16 + 8) * slots + s, 8, stride=slots), :]
-                at = tile_at[s] * (width // 8) + g
-                if m == 0:
-                    added = jnp.where(low, a, pltpu.roll(c, HALF, 1))
-                else:
-                    added = jnp.where(low, pltpu.roll(a, HALF, 1), c)
-                ens_v[m, at] = ens_v[m, at] + added
+        for p, size in enumerate(parts):
+            for r in range(size):
+                for g in range(4):
+                    row = bases[p] + g * 16 * size + r
+                    a = back_v[pl.ds(row, 8, stride=size), :]
+                    c = back_v[pl.ds(row + 8 * size, 8, stride=size), :]
+                    at = tile_at[firsts[p] + r] * (width // 8) + g
+                    if m == 0:
+                        added = jnp.where(low, a, pltpu.roll(c, HALF, 1))
+                    else:
+                        added = jnp.where(low, pltpu.roll(a, HALF, 1), c)
+                    ens_v[m, at] = ens_v[m, at] + added
         store = pltpu.make_async_copy(ens_v.at[m], out_ref.at[m], sems.at[4 + m])
         store.start()
         stores.append(store)
@@ -427,7 +436,8 @@
 
 
 def filter_tiles(cfg, ens, obs_sites, owner, obs_values, obs_error):
-    levels, count, slots, tiles, width, blocks, obs = cfg
+    levels, count, parts, tiles, width, blocks, obs = cfg
+    slots = sum(parts)
     n_obs = blocks * obs
     hbm = pl.BlockSpec(memory_space=pltpu.HBM)
     anywhere = pl.BlockSpec(memory_space=pl.ANY)
@@ -461,11 +471,11 @@
             dma((levels,)),
             dma,
             dma,
-            dma,
-            dma,
-            dma,
-            dma,
-            dma,
+            dma((len(parts),)),
+            dma((len(parts),)),
+            dma((len(parts),)),
+            dma((len(parts),)),
+            dma((len(parts),)),
         ],
         compiler_params=pltpu.CompilerParams(
             collective_id=slots, has_side_effects=True, vmem_limit_bytes=limit
@@ -486,7 +496,7 @@
     )(owner, ens, back)
 
 
-def shards(sizes, ensemble, obs_sites, owner, tile_mask, obs_values, obs_error):
+def shards(layouts, ensemble, obs_sites, owner, tile_mask, obs_values, obs_error):
     levels, count = lax.axis_size("lev"), lax.axis_size("var")
     _, m_dev, x_all, y_all = ensemble.shape
     blocks, obs = obs_sites.shape
@@ -494,14 +504,14 @@
     ens = ensemble.reshape(m_dev, x_all // 8, 8, y_all)
     rest = (ens, obs_sites, owner, obs_values, obs_error)
     branches = [
-        functools.partial(filter_tiles, (levels, count, n, tiles, x_all // tiles, blocks, obs))
-        for n in sizes
+        functools.partial(filter_tiles, (levels, count, parts, tiles, x_all // tiles, blocks, obs))
+        for parts in layouts
     ]
-    if len(sizes) == 1:
+    if len(layouts) == 1:
         out = branches[0](*rest)
     else:
         touched = jnp.sum(jnp.max(tile_mask, axis=0))
-        which = sum((touched > n).astype(jnp.int32) for n in sizes[:-1])
+        which = sum((touched > sum(parts)).astype(jnp.int32) for parts in layouts[:-1])
         out = lax.switch(which, branches, *rest)
     return out.reshape(ensemble.shape)
 
@@ -510,7 +520,7 @@
     in_specs = (P("lev", "var", None, None), P(), P(), P(), P(), P())
     out_specs = P("lev", "var", None, None)
     return jax.shard_map(
-        functools.partial(shards, SIZES),
+        functools.partial(shards, LAYOUTS),
         mesh=mesh,
         in_specs=in_specs,
         out_specs=out_specs,

time: 56.2 us -> 52.4 us (0.932)
  Pallas kernels: 54 us -> 50.2 us
    pallas_call x1, Pallas kernels: 51 us -> 47.2 us  [filter_tiles(): pl.pallas_call(functools.partial(exchange_kernel, cfg), out_shape=jax.Sha...]
where the time goes in v4:
time: 52.4 us; the launch traced here: 52.3 us
  Pallas kernels  50.2 us (96%)
  other arithmetic  1.33 us (3%)
  between operations  0.66 us (1%)
    pallas_call x1, Pallas kernels, filter_tiles(): pl.pallas_call(functools.partial(exchange_kernel, cfg), out_shape=jax.Sha...  47.2 us
    pallas_call x1, Pallas kernels, filter_tiles(): pl.pallas_call(functools.partial(apply_kernel, cfg), out_shape=jax.ShapeD...  3 us

profile of v4, /device:TPU:1, one launch (start us, length us, event | category | flops | bytes accessed | tf_op | source)
XLA Modules:
  0.0 52.3 jit_solution(3076302121828534700)
XLA Ops:
  0.0 0.7 %reduce_max.9 = s32[64]{0:T(128)S(1)} reduce(s32[4,64]{1,0:T(4,128)} %param.11, s32[]{:T(128)} %constant.1.clone.1), dimensions={0}, to_apply=%region_0.0 | reduce | flops 192 | bytes 1284 | tf_op jit(solution)/shard_map/reduce_max | solution.py:513
  0.7 0.6 %reduce_sum.9 = s32[]{:T(128)} reduce(s32[64]{0:T(128)S(1)} %reduce_max.9, s32[]{:T(128)} %constant.0.clone.1), dimensions={0}, to_apply=%region_1.0 | reduce | flops 63 | bytes 264 | tf_op jit(solution)/shard_map/reduce_sum | solution.py:513
  2.0 50.3 %conditional.1 = (f32[1,2,2048,128]{3,2,1,0:T(8,128)}) conditional(s32[]{:T(128)} %clamp.3, (s32[4,8]{1,0:T(4,128)}, s32[4]{0:T(128)}, f32[4,8]{1,0:T(4,128)}, f32[4,8]{1,0:T(4,128)}, f32[2,256,8,128]{3,2,1,0:T(8,128)}) %tuple.18, (s32[4,8]{1,0:T(4,128)}, s32[4]{0:T(128)}, f32[4,8]{1,0:T(4,128)}, f32[4,8]{1,0:T(4,128)}, ...), branch_computations={%region_2.0_spmd, %region_3.0_spmd} | conditional | bytes 100 | solution.py:515
  2.0 0.0 copy-start
  2.0 47.2 %branch_0_fun.2.back_ref = f32[1408,128]{1,0:T(8,128)} custom-call(s32[4,8]{1,0:T(4,128)} %get-tuple-element.31.sites_hbm, s32[4]{0:T(128)} %get-tuple-element.29.owner_hbm, f32[4,8]{1,0:T(4,128)} %get-tuple-element.32.values_hbm, f32[4,8]{1,0:T(4,128)} %get-tuple-element.33.errors_hbm, f32[2,256,8,128]{3,2,1,0:T(8,128)} %get-tuple-element.30.ens_ref), custom_call_target="tpu_custom_call" | custom-call | tf_op jit(solution)/shard_map/cond/branch_0_fun/pallas_call | solution.py:446
  49.2 0.0 copy-done
  49.3 3.0 %branch_0_fun.3 = f32[2,256,8,128]{3,2,1,0:T(8,128)} custom-call(s32[4]{0:T(128)S(1)} %copy-done, f32[2,256,8,128]{3,2,1,0:T(8,128)} %get-tuple-element.30.ens_ref, f32[1408,128]{1,0:T(8,128)} %branch_0_fun.2.back_ref), custom_call_target="tpu_custom_call" | custom-call | tf_op jit(solution)/shard_map/cond/branch_0_fun/pallas_call | solution.py:484
Async XLA Ops:
  2.0 47.2 %copy-start = (s32[4]{0:T(128)S(1)}, s32[4]{0:T(128)}, u32[]{:S(2)}) copy-start(s32[4]{0:T(128)} %get-tuple-element.29.owner_hbm) | copy-start | bytes 52 | tf_op jit(solution)/shard_map/cond

commit v5 on v4

--- a/solution.py
+++ b/solution.py
@@ -11,7 +11,8 @@
 HIGHEST = lax.Precision.HIGHEST
 F32 = jnp.float32
 REACH = 3
-LAYOUTS = ((8, 14), (10, 18))
+PARTS = (8, 14)
+MORE_PARTS = (6,)
 VMEM_BYTES = 64 * 2**20
 HALF = 64
 
@@ -20,25 +21,25 @@
     return jnp.minimum(jnp.maximum(value - edge + 1, 0), 1)
 
 
-def changed_tiles(owner_ref, blocks, tiles, slots):
+def changed_tiles(owner_ref, blocks, tiles, start, slots):
     t = [owner_ref[b] & (tiles - 1) for b in range(blocks)]
     for i in range(blocks):
         for j in range(blocks - 1 - i):
             t[j], t[j + 1] = jnp.minimum(t[j], t[j + 1]), jnp.maximum(t[j], t[j + 1])
     befores, gaps, total, end = [], [], 0, -1
     for b in range(blocks):
-        start = jnp.maximum(jnp.maximum(t[b] - REACH, end + 1), 0)
-        gaps.append(start - end - 1)
+        begin = jnp.maximum(jnp.maximum(t[b] - REACH, end + 1), 0)
+        gaps.append(begin - end - 1)
         end = jnp.minimum(t[b] + REACH, tiles - 1)
         befores.append(total)
-        total = total + jnp.maximum(end - start + 1, 0)
+        total = total + jnp.maximum(end - begin + 1, 0)
     found = []
-    for s in range(slots):
+    for s in range(start, start + slots):
         tile = gaps[0] + s
         for b in range(1, blocks):
             tile = tile + gaps[b] * step_at(s, befores[b])
         found.append((tile + 1) * step_at(total - 1, s) - 1)
-    return found
+    return found, total
 
 
 def places(parts, count):
@@ -58,10 +59,12 @@
     errors_hbm,
     ens_ref,
     back_ref,
+    more_hbm,
     sites_ref,
     owner_ref,
     values_ref,
     errors_ref,
+    more_ref,
     ens_v,
     out_buf,
     in_buf,
@@ -76,6 +79,7 @@
     r_v,
     load_sem,
     small_sem,
+    more_sem,
     near_send,
     near_recv,
     row_send,
@@ -86,7 +90,7 @@
     ret_recv,
     own_sem,
 ):
-    levels, count, parts, tiles, width, blocks, obs = cfg
+    levels, count, start, parts, tiles, width, blocks, obs = cfg
     slots = sum(parts)
     n_obs = blocks * obs
     members = 2 * count
@@ -131,7 +135,10 @@
 
     lane = lax.broadcasted_iota(jnp.int32, (1, 128), 1)
     low = lane < HALF
-    tile_at = changed_tiles(owner_ref, blocks, tiles, slots)
+    tile_at, touched = changed_tiles(owner_ref, blocks, tiles, start, slots)
+    more_ref[0] = step_at(touched - 1, start + slots)
+    tell = pltpu.make_async_copy(more_ref, more_hbm, more_sem)
+    tell.start()
 
     load.wait()
 
@@ -385,6 +392,7 @@
         copy.start()
         own.append(copy)
 
+    tell.wait()
     rows = row_in.at[pl.ds(0, count - 1)]
     pltpu.make_async_copy(rows, rows, row_send).wait()
     for p in range(len(parts)):
@@ -396,63 +404,78 @@
         wait_part(p, ret_buf, ret_send)
 
 
-def apply_kernel(cfg, owner_hbm, ens_ref, back_ref, out_ref, owner_ref, ens_v, back_v, sems):
-    levels, count, parts, tiles, width, blocks, obs = cfg
-    slots = sum(parts)
+def apply_kernel(cfgs, owner_hbm, ens_ref, *refs):
+    n = len(cfgs)
+    backs, out_ref, owner_ref, ens_v, kept, sems = (
+        refs[:n],
+        refs[n],
+        refs[n + 1],
+        refs[n + 2],
+        refs[n + 3 : 2 * n + 3],
+        refs[2 * n + 3],
+    )
     small = pltpu.make_async_copy(owner_hbm, owner_ref, sems.at[0])
     small.start()
-    firsts, bases = places(parts, count)
-    load_back = pltpu.make_async_copy(back_ref, back_v, sems.at[1])
-    load_back.start()
+    load_backs = [
+        pltpu.make_async_copy(backs[i], kept[i], sems.at[5 + i]) for i in range(n)
+    ]
     loads = [
-        pltpu.make_async_copy(ens_ref.at[m], ens_v.at[m], sems.at[2 + m]) for m in range(2)
+        pltpu.make_async_copy(ens_ref.at[m], ens_v.at[m], sems.at[1 + m]) for m in range(2)
     ]
-    for load in loads:
+    for load in load_backs + loads:
         load.start()
     small.wait()
-    tile_at = [jnp.maximum(t, 0) for t in changed_tiles(owner_ref, blocks, tiles, slots)]
     low = lax.broadcasted_iota(jnp.int32, (1, 128), 1) < HALF
-    load_back.wait()
+    for load in load_backs:
+        load.wait()
     stores = []
     for m in range(2):
         loads[m].wait()
-        for p, size in enumerate(parts):
-            for r in range(size):
-                for g in range(4):
-                    row = bases[p] + g * 16 * size + r
-                    a = back_v[pl.ds(row, 8, stride=size), :]
-                    c = back_v[pl.ds(row + 8 * size, 8, stride=size), :]
-                    at = tile_at[firsts[p] + r] * (width // 8) + g
-                    if m == 0:
-                        added = jnp.where(low, a, pltpu.roll(c, HALF, 1))
-                    else:
-                        added = jnp.where(low, pltpu.roll(a, HALF, 1), c)
-                    ens_v[m, at] = ens_v[m, at] + added
-        store = pltpu.make_async_copy(ens_v.at[m], out_ref.at[m], sems.at[4 + m])
+        for i, (levels, count, start, parts, tiles, width, blocks, obs) in enumerate(cfgs):
+            firsts, bases = places(parts, count)
+            tile_at, _ = changed_tiles(owner_ref, blocks, tiles, start, sum(parts))
+            for p, size in enumerate(parts):
+                for r in range(size):
+                    tile = jnp.maximum(tile_at[firsts[p] + r], 0)
+                    for g in range(4):
+                        row = bases[p] + g * 16 * size + r
+                        a = kept[i][pl.ds(row, 8, stride=size), :]
+                        c = kept[i][pl.ds(row + 8 * size, 8, stride=size), :]
+                        at = tile * (width // 8) + g
+                        if m == 0:
+                            added = jnp.where(low, a, pltpu.roll(c, HALF, 1))
+                        else:
+                            added = jnp.where(low, pltpu.roll(a, HALF, 1), c)
+                        ens_v[m, at] = ens_v[m, at] + added
+        store = pltpu.make_async_copy(ens_v.at[m], out_ref.at[m], sems.at[3 + m])
         store.start()
         stores.append(store)
     for store in stores:
         store.wait()
 
 
-def filter_tiles(cfg, ens, obs_sites, owner, obs_values, obs_error):
-    levels, count, parts, tiles, width, blocks, obs = cfg
+def exchange(cfg, ens, obs_sites, owner, obs_values, obs_error):
+    levels, count, start, parts, tiles, width, blocks, obs = cfg
     slots = sum(parts)
     n_obs = blocks * obs
     hbm = pl.BlockSpec(memory_space=pltpu.HBM)
     anywhere = pl.BlockSpec(memory_space=pl.ANY)
     dma = pltpu.SemaphoreType.DMA
     limit = VMEM_BYTES - 4 * count * slots * 128
-    back = pl.pallas_call(
+    return pl.pallas_call(
         functools.partial(exchange_kernel, cfg),
-        out_shape=jax.ShapeDtypeStruct((count * slots, 128), F32),
+        out_shape=(
+            jax.ShapeDtypeStruct((count * slots, 128), F32),
+            jax.ShapeDtypeStruct((1,), jnp.int32),
+        ),
         in_specs=[hbm] * 5,
-        out_specs=anywhere,
+        out_specs=(anywhere, hbm),
         scratch_shapes=[
             pltpu.SMEM(obs_sites.shape, jnp.int32),
             pltpu.SMEM(owner.shape, jnp.int32),
             pltpu.SMEM(obs_values.shape, F32),
             pltpu.SMEM(obs_error.shape, F32),
+            pltpu.SMEM((1,), jnp.int32),
             pltpu.VMEM(ens.shape, F32),
             pltpu.VMEM((count * slots, 128), F32),
             pltpu.VMEM((count * slots, 128), F32),
@@ -467,6 +490,7 @@
             pltpu.VMEM((slots // 2, n_obs, 128), F32),
             dma,
             dma((4,)),
+            dma,
             dma((levels,)),
             dma((levels,)),
             dma,
@@ -478,41 +502,48 @@
             dma((len(parts),)),
         ],
         compiler_params=pltpu.CompilerParams(
-            collective_id=slots, has_side_effects=True, vmem_limit_bytes=limit
+            collective_id=1 + start, has_side_effects=True, vmem_limit_bytes=limit
         ),
     )(obs_sites, owner, obs_values, obs_error, ens)
+
+
+def apply(cfgs, owner, ens, *backs):
+    hbm = pl.BlockSpec(memory_space=pltpu.HBM)
+    anywhere = pl.BlockSpec(memory_space=pl.ANY)
+    dma = pltpu.SemaphoreType.DMA
     return pl.pallas_call(
-        functools.partial(apply_kernel, cfg),
+        functools.partial(apply_kernel, cfgs),
         out_shape=jax.ShapeDtypeStruct(ens.shape, F32),
-        in_specs=[hbm, hbm, anywhere],
+        in_specs=[hbm, hbm] + [anywhere] * len(backs),
         out_specs=hbm,
         scratch_shapes=[
             pltpu.SMEM(owner.shape, jnp.int32),
             pltpu.VMEM(ens.shape, F32),
-            pltpu.VMEM((count * slots, 128), F32),
-            dma((6,)),
+            *[pltpu.VMEM(back.shape, F32) for back in backs],
+            dma((5 + len(backs),)),
         ],
-        compiler_params=pltpu.CompilerParams(vmem_limit_bytes=limit),
-    )(owner, ens, back)
-
-
-def shards(layouts, ensemble, obs_sites, owner, tile_mask, obs_values, obs_error):
+        compiler_params=pltpu.CompilerParams(
+            vmem_limit_bytes=VMEM_BYTES - 4 * sum(back.size for back in backs)
+        ),
+    )(owner, ens, *backs)
+
+
+def shards(ensemble, obs_sites, owner, tile_mask, obs_values, obs_error):
     levels, count = lax.axis_size("lev"), lax.axis_size("var")
     _, m_dev, x_all, y_all = ensemble.shape
     blocks, obs = obs_sites.shape
     tiles = tile_mask.shape[1]
     ens = ensemble.reshape(m_dev, x_all // 8, 8, y_all)
-    rest = (ens, obs_sites, owner, obs_values, obs_error)
-    branches = [
-        functools.partial(filter_tiles, (levels, count, parts, tiles, x_all // tiles, blocks, obs))
-        for parts in layouts
-    ]
-    if len(layouts) == 1:
-        out = branches[0](*rest)
-    else:
-        touched = jnp.sum(jnp.max(tile_mask, axis=0))
-        which = sum((touched > sum(parts)).astype(jnp.int32) for parts in layouts[:-1])
-        out = lax.switch(which, branches, *rest)
+    here = (tiles, x_all // tiles, blocks, obs)
+    cfg = (levels, count, 0, PARTS, *here)
+    more_cfg = (levels, count, sum(PARTS), MORE_PARTS, *here)
+    back, more = exchange(cfg, ens, obs_sites, owner, obs_values, obs_error)
+
+    def with_more():
+        more_back, _ = exchange(more_cfg, ens, obs_sites, owner, obs_values, obs_error)
+        return apply((cfg, more_cfg), owner, ens, back, more_back)
+
+    out = lax.cond(more[0] > 0, with_more, lambda: apply((cfg,), owner, ens, back))
     return out.reshape(ensemble.shape)
 
 
@@ -520,7 +551,7 @@
     in_specs = (P("lev", "var", None, None), P(), P(), P(), P(), P())
     out_specs = P("lev", "var", None, None)
     return jax.shard_map(
-        functools.partial(shards, LAYOUTS),
+        shards,
         mesh=mesh,
         in_specs=in_specs,
         out_specs=out_specs,

time: 52.4 us -> 51.1 us (0.975)
  other arithmetic: 1.33 us -> 0 us
    reduce_max x1 -> x0, other arithmetic: 0.7 us -> none  [shards(): touched = jnp.sum(jnp.max(tile_mask, axis=0))]
    reduce_sum x1 -> x0, other arithmetic: 0.63 us -> none  [shards(): touched = jnp.sum(jnp.max(tile_mask, axis=0))]
where the time goes in v5:
time: 51.1 us; the launch traced here: 51 us
  Pallas kernels  50.3 us (98%)
  between operations  0.67 us (1%)
    pallas_call x1, Pallas kernels, exchange(): pl.pallas_call(functools.partial(exchange_kernel, cfg), out_shape=(jax.Sh...  47.2 us
    pallas_call x1, Pallas kernels, apply(): pl.pallas_call(functools.partial(apply_kernel, cfgs), out_shape=jax.Shape...  3.07 us

profile of v5, /device:TPU:1, one launch (start us, length us, event | category | flops | bytes accessed | tf_op | source)
XLA Modules:
  0.0 51.0 jit_solution(2783611014716235448)
XLA Ops:
  0.0 0.0 copy-start.3
  0.0 0.0 copy-start.2
  0.0 0.0 copy-start.1
  0.0 0.0 copy-start
  0.0 47.2 %shard_map.57 = (f32[1408,128]{1,0:T(8,128)}, s32[1]{0:T(128)}) custom-call(s32[4,8]{1,0:T(4,128)} %sites_hbm.1, s32[4]{0:T(128)} %owner_hbm.1, f32[4,8]{1,0:T(4,128)} %values_hbm.1, f32[4,8]{1,0:T(4,128)} %errors_hbm.1, f32[2,256,8,128]{3,2,1,0:T(8,128)} %bitcast.4), custom_call_target="tpu_custom_call" | custom-call | tf_op jit(solution)/shard_map/pallas_call | solution.py:465
  47.9 0.0 copy-done.3
  47.9 0.0 copy-done.2
  47.9 0.0 copy-done.1
  47.9 0.0 copy-done
  47.9 3.1 %conditional.1 = (f32[1,2,2048,128]{3,2,1,0:T(8,128)}) conditional(s32[]{:T(128)} %bitcast.3, (s32[4]{0:T(128)S(1)}, f32[2,256,8,128]{3,2,1,0:T(8,128)}, f32[1408,128]{1,0:T(8,128)}) %tuple.24, (s32[4,8]{1,0:T(4,128)S(1)}, s32[4]{0:T(128)S(1)}, f32[4,8]{1,0:T(4,128)S(1)}, f32[4,8]{1,0:T(4,128)S(1)}, f32[2,256,8,128]{3,2,1,0:T(8,128)}, ...), branch_computations={%region_0.0_spmd, %region_1.0_spmd} | conditional | bytes 8 | solution.py:546
  47.9 3.1 %branch_0_fun.1 = f32[2,256,8,128]{3,2,1,0:T(8,128)} custom-call(s32[4]{0:T(128)S(1)} %get-tuple-element.27.owner_hbm, f32[2,256,8,128]{3,2,1,0:T(8,128)} %get-tuple-element.28.ens_ref, f32[1408,128]{1,0:T(8,128)} %get-tuple-element.29.refs_0_), custom_call_target="tpu_custom_call" | custom-call | tf_op jit(solution)/shard_map/cond/branch_0_fun/pallas_call | solution.py:514
Async XLA Ops:
  0.0 47.9 %copy-start.3 = (s32[4]{0:T(128)S(1)}, s32[4]{0:T(128)}, u32[]{:S(2)}) copy-start(s32[4]{0:T(128)} %owner_hbm.1) | copy-start | bytes 52
  0.0 47.9 %copy-start.2 = (f32[4,8]{1,0:T(4,128)S(1)}, f32[4,8]{1,0:T(4,128)}, u32[]{:S(2)}) copy-start(f32[4,8]{1,0:T(4,128)} %errors_hbm.1) | copy-start | bytes 388
  0.0 47.9 %copy-start.1 = (f32[4,8]{1,0:T(4,128)S(1)}, f32[4,8]{1,0:T(4,128)}, u32[]{:S(2)}) copy-start(f32[4,8]{1,0:T(4,128)} %values_hbm.1) | copy-start | bytes 388
  0.0 47.9 %copy-start = (s32[4,8]{1,0:T(4,128)S(1)}, s32[4,8]{1,0:T(4,128)}, u32[]{:S(2)}) copy-start(s32[4,8]{1,0:T(4,128)} %sites_hbm.1) | copy-start | bytes 388

commit v6 on v5

--- a/solution.py
+++ b/solution.py
@@ -157,7 +157,8 @@
     mine = jnp.sum(jnp.where(sub64 == lane64, sums, 0.0), axis=0, keepdims=True)
     near_buf[pl.ds(0, 8), :] = jnp.broadcast_to(mine, (8, 128))
 
-    for p, size in enumerate(parts):
+    def lay_out(p):
+        size = parts[p]
         for r in range(size):
             tile = jnp.maximum(tile_at[firsts[p] + r], 0)
             for g in range(4):
@@ -205,7 +206,10 @@
         rest = pl.ds(bases[p], (count - 1) * parts[p])
         pltpu.make_async_copy(buf.at[rest], buf.at[rest], sem.at[p]).wait()
 
+    lay_out(0)
     send_part(0, out_buf, in_buf, bulk_send, bulk_recv)
+    for p in range(1, len(parts)):
+        lay_out(p)
     for copy in near:
         copy.wait_recv()
     row_buf[...] = (near_buf[pl.ds(0, 8), :] + near_buf[pl.ds(8, 8), :]) + (

time: 51.1 us -> 50.9 us (level)
  no operation moved by 1% of the time
where the time goes in v6:
time: 50.9 us; the launch traced here: 50.8 us
  Pallas kernels  50.1 us (98%)
  between operations  0.67 us (1%)
    pallas_call x1, Pallas kernels, exchange(): pl.pallas_call(functools.partial(exchange_kernel, cfg), out_shape=(jax.Sh...  47 us
    pallas_call x1, Pallas kernels, apply(): pl.pallas_call(functools.partial(apply_kernel, cfgs), out_shape=jax.Shape...  3.07 us

profile of v6, /device:TPU:1, one launch (start us, length us, event | category | flops | bytes accessed | tf_op | source)
XLA Modules:
  0.0 50.8 jit_solution(17328191069962796056)
XLA Ops:
  0.0 0.0 copy-start.3
  0.0 0.0 copy-start.2
  0.0 0.0 copy-start.1
  0.0 0.0 copy-start
  0.0 47.0 %shard_map.57 = (f32[1408,128]{1,0:T(8,128)}, s32[1]{0:T(128)}) custom-call(s32[4,8]{1,0:T(4,128)} %sites_hbm.1, s32[4]{0:T(128)} %owner_hbm.1, f32[4,8]{1,0:T(4,128)} %values_hbm.1, f32[4,8]{1,0:T(4,128)} %errors_hbm.1, f32[2,256,8,128]{3,2,1,0:T(8,128)} %bitcast.4), custom_call_target="tpu_custom_call" | custom-call | tf_op jit(solution)/shard_map/pallas_call | solution.py:469
  47.6 0.0 copy-done.3
  47.6 0.0 copy-done.2
  47.7 0.0 copy-done.1
  47.7 0.0 copy-done
  47.7 3.1 %conditional.1 = (f32[1,2,2048,128]{3,2,1,0:T(8,128)}) conditional(s32[]{:T(128)} %bitcast.3, (s32[4]{0:T(128)S(1)}, f32[2,256,8,128]{3,2,1,0:T(8,128)}, f32[1408,128]{1,0:T(8,128)}) %tuple.24, (s32[4,8]{1,0:T(4,128)S(1)}, s32[4]{0:T(128)S(1)}, f32[4,8]{1,0:T(4,128)S(1)}, f32[4,8]{1,0:T(4,128)S(1)}, f32[2,256,8,128]{3,2,1,0:T(8,128)}, ...), branch_computations={%region_0.0_spmd, %region_1.0_spmd} | conditional | bytes 8 | solution.py:550
  47.7 3.1 %branch_0_fun.1 = f32[2,256,8,128]{3,2,1,0:T(8,128)} custom-call(s32[4]{0:T(128)S(1)} %get-tuple-element.27.owner_hbm, f32[2,256,8,128]{3,2,1,0:T(8,128)} %get-tuple-element.28.ens_ref, f32[1408,128]{1,0:T(8,128)} %get-tuple-element.29.refs_0_), custom_call_target="tpu_custom_call" | custom-call | tf_op jit(solution)/shard_map/cond/branch_0_fun/pallas_call | solution.py:518
Async XLA Ops:
  0.0 47.6 %copy-start.3 = (s32[4]{0:T(128)S(1)}, s32[4]{0:T(128)}, u32[]{:S(2)}) copy-start(s32[4]{0:T(128)} %owner_hbm.1) | copy-start | bytes 52
  0.0 47.6 %copy-start.2 = (f32[4,8]{1,0:T(4,128)S(1)}, f32[4,8]{1,0:T(4,128)}, u32[]{:S(2)}) copy-start(f32[4,8]{1,0:T(4,128)} %errors_hbm.1) | copy-start | bytes 388
  0.0 47.7 %copy-start.1 = (f32[4,8]{1,0:T(4,128)S(1)}, f32[4,8]{1,0:T(4,128)}, u32[]{:S(2)}) copy-start(f32[4,8]{1,0:T(4,128)} %values_hbm.1) | copy-start | bytes 388
  0.0 47.7 %copy-start = (s32[4,8]{1,0:T(4,128)S(1)}, s32[4,8]{1,0:T(4,128)}, u32[]{:S(2)}) copy-start(s32[4,8]{1,0:T(4,128)} %sites_hbm.1) | copy-start | bytes 388

commit v7 on v5

--- a/solution.py
+++ b/solution.py
@@ -11,7 +11,7 @@
 HIGHEST = lax.Precision.HIGHEST
 F32 = jnp.float32
 REACH = 3
-PARTS = (8, 14)
+PARTS = (6, 8, 8)
 MORE_PARTS = (6,)
 VMEM_BYTES = 64 * 2**20
 HALF = 64
@@ -157,18 +157,6 @@
     mine = jnp.sum(jnp.where(sub64 == lane64, sums, 0.0), axis=0, keepdims=True)
     near_buf[pl.ds(0, 8), :] = jnp.broadcast_to(mine, (8, 128))
 
-    for p, size in enumerate(parts):
-        for r in range(size):
-            tile = jnp.maximum(tile_at[firsts[p] + r], 0)
-            for g in range(4):
-                a = ens_v[0, tile * (width // 8) + g]
-                c = ens_v[1, tile * (width // 8) + g]
-                row = bases[p] + g * 16 * size + r
-                out_buf[pl.ds(row, 8, stride=size), :] = jnp.where(low, a, pltpu.roll(c, HALF, 1))
-                out_buf[pl.ds(row + 8 * size, 8, stride=size), :] = jnp.where(
-                    low, pltpu.roll(a, HALF, 1), c
-                )
-
     pl.semaphore_wait(barrier, count - 1 + levels - 1)
 
     near = []
@@ -183,6 +171,18 @@
         )
         copy.start()
         near.append(copy)
+
+    for p, size in enumerate(parts):
+        for r in range(size):
+            tile = jnp.maximum(tile_at[firsts[p] + r], 0)
+            for g in range(4):
+                a = ens_v[0, tile * (width // 8) + g]
+                c = ens_v[1, tile * (width // 8) + g]
+                row = bases[p] + g * 16 * size + r
+                out_buf[pl.ds(row, 8, stride=size), :] = jnp.where(low, a, pltpu.roll(c, HALF, 1))
+                out_buf[pl.ds(row + 8 * size, 8, stride=size), :] = jnp.where(
+                    low, pltpu.roll(a, HALF, 1), c
+                )
 
     def send_part(p, src, dst, send_sem, recv_sem):
         size = parts[p]

time: 51.1 us -> 50.8 us (level)
  no operation moved by 1% of the time
where the time goes in v7:
time: 50.8 us; the launch traced here: 50.6 us
  Pallas kernels  49.9 us (98%)
  between operations  0.67 us (1%)
    pallas_call x1, Pallas kernels, exchange(): pl.pallas_call(functools.partial(exchange_kernel, cfg), out_shape=(jax.Sh...  46.9 us
    pallas_call x1, Pallas kernels, apply(): pl.pallas_call(functools.partial(apply_kernel, cfgs), out_shape=jax.Shape...  3.07 us

profile of v7, /device:TPU:1, one launch (start us, length us, event | category | flops | bytes accessed | tf_op | source)
XLA Modules:
  0.0 50.6 jit_solution(3597152622720486558)
XLA Ops:
  0.0 0.0 copy-start.3
  0.0 0.0 copy-start.2
  0.0 0.0 copy-start.1
  0.0 0.0 copy-start
  0.0 46.9 %shard_map.57 = (f32[1408,128]{1,0:T(8,128)}, s32[1]{0:T(128)}) custom-call(s32[4,8]{1,0:T(4,128)} %sites_hbm.1, s32[4]{0:T(128)} %owner_hbm.1, f32[4,8]{1,0:T(4,128)} %values_hbm.1, f32[4,8]{1,0:T(4,128)} %errors_hbm.1, f32[2,256,8,128]{3,2,1,0:T(8,128)} %bitcast.4), custom_call_target="tpu_custom_call" | custom-call | tf_op jit(solution)/shard_map/pallas_call | solution.py:465
  47.5 0.0 copy-done.3
  47.5 0.0 copy-done.2
  47.5 0.0 copy-done.1
  47.5 0.0 copy-done
  47.6 3.1 %conditional.1 = (f32[1,2,2048,128]{3,2,1,0:T(8,128)}) conditional(s32[]{:T(128)} %bitcast.3, (s32[4]{0:T(128)S(1)}, f32[2,256,8,128]{3,2,1,0:T(8,128)}, f32[1408,128]{1,0:T(8,128)}) %tuple.24, (s32[4,8]{1,0:T(4,128)S(1)}, s32[4]{0:T(128)S(1)}, f32[4,8]{1,0:T(4,128)S(1)}, f32[4,8]{1,0:T(4,128)S(1)}, f32[2,256,8,128]{3,2,1,0:T(8,128)}, ...), branch_computations={%region_0.0_spmd, %region_1.0_spmd} | conditional | bytes 8 | solution.py:546
  47.6 3.1 %branch_0_fun.1 = f32[2,256,8,128]{3,2,1,0:T(8,128)} custom-call(s32[4]{0:T(128)S(1)} %get-tuple-element.27.owner_hbm, f32[2,256,8,128]{3,2,1,0:T(8,128)} %get-tuple-element.28.ens_ref, f32[1408,128]{1,0:T(8,128)} %get-tuple-element.29.refs_0_), custom_call_target="tpu_custom_call" | custom-call | tf_op jit(solution)/shard_map/cond/branch_0_fun/pallas_call | solution.py:514
Async XLA Ops:
  0.0 47.5 %copy-start.3 = (s32[4]{0:T(128)S(1)}, s32[4]{0:T(128)}, u32[]{:S(2)}) copy-start(s32[4]{0:T(128)} %owner_hbm.1) | copy-start | bytes 52
  0.0 47.5 %copy-start.2 = (f32[4,8]{1,0:T(4,128)S(1)}, f32[4,8]{1,0:T(4,128)}, u32[]{:S(2)}) copy-start(f32[4,8]{1,0:T(4,128)} %errors_hbm.1) | copy-start | bytes 388
  0.0 47.5 %copy-start.1 = (f32[4,8]{1,0:T(4,128)S(1)}, f32[4,8]{1,0:T(4,128)}, u32[]{:S(2)}) copy-start(f32[4,8]{1,0:T(4,128)} %values_hbm.1) | copy-start | bytes 388
  0.0 47.5 %copy-start = (s32[4,8]{1,0:T(4,128)S(1)}, s32[4,8]{1,0:T(4,128)}, u32[]{:S(2)}) copy-start(s32[4,8]{1,0:T(4,128)} %sites_hbm.1) | copy-start | bytes 388
